TPU v7x, 32 devices: a whole 2x2x4 slice. The times are simulated.
32 devices in a mesh: draws: 2 (over x), spec: 16 (over z, y, core).
Axes of the slice: x: 2, y: 2, z: 4, core: 2. Of those that a mesh axis runs over, the one named last changes fastest.
Arguments:
- coefficients: bfloat16 [1280, 2, 320, 128], P('draws', None, 'spec'), parts along dimension 0, may hold values from -6 to 6
- legendre: float32 [640, 2, 320, 16], P('spec'), as said below
- row_counts: int32 [16], P('spec'), may hold values from 640 to 1280, as said below
- basis: float32 [64, 128], replicated, may hold values from -0.75 to 0.75
- absorb: float32 [128], replicated, may hold values from 0.00390625 to 0.0625
- peak_level: int32 [512], replicated, may hold values from 0 to 127
- width: float32 [512], replicated, may hold values from 1.5 to 12
Outputs:
- radiance: float32 [32, 2, 1280, 512], P(('draws', 'spec')), parts along dimension 0
There are 2 independent parts, one for each index of `draws`. A program takes and returns all parts, laid end to end along the dimension named above; an argument that names none is the same for every part. Nothing has to cross between parts.
Inputs may be any that keep to these rules, and one draw needn't show every extreme that they name: `legendre`: entry [m, p, s, j] is the associated Legendre function of order m and degree m + 2 s + p, normalised to unit square integral over [-1, 1], at the cosine of a drawn colatitude of row j in the northern hemisphere; it is zero where the degree exceeds 640 - 1. `row_counts`: every count is a multiple of 4; row 0 has 1280 longitudes and row 1 has 640.
All inputs are finite; a program needn't handle non-finite values.
Results may differ from a plain program's by a relative error of at most 0.0003.
Values sent between devices are 32-bit elements; how exact they have to be, the bound alone decides.
No kernel may reach another device: no remote copies, remote signals or barrier semaphores. Data moves between devices by JAX's collectives and lax.ppermute only.
A program may use at most 128 MiB of HBM per device.

v0:
```python
import math

import jax
import jax.numpy as jnp
from jax import lax
from jax.sharding import PartitionSpec as P

NLON = 1280


PRECISE = lax.Precision.HIGHEST


def prior_scale(shard, first):
    waves = shard.shape[0]
    slots = shard.shape[2]
    orders = jnp.arange(waves, dtype=jnp.int32)[:, None, None]
    parity = jnp.arange(2, dtype=jnp.int32)[None, :, None]
    slot_index = first + jnp.arange(slots, dtype=jnp.int32)[None, None, :]
    degree = orders + 2 * slot_index + parity
    spread = lax.rsqrt((degree + 1).astype(jnp.float32) * waves)
    spread = jnp.where(degree < waves, spread, jnp.zeros_like(spread))
    return shard.astype(jnp.float32) * spread[..., None]


def channel_kernel(peak_level, width, levels):
    height = jnp.arange(levels, dtype=jnp.float32)[:, None]
    offsets = (height - peak_level.astype(jnp.float32)[None, :]) / width[None, :]
    weights = jnp.exp(-offsets * offsets)
    return weights / jnp.sum(weights, axis=0, keepdims=True)


def radiate(temps, absorb, kernel):
    levels = temps.shape[-1]
    strict_upper = (jnp.arange(levels)[:, None] < jnp.arange(levels)[None, :]).astype(jnp.float32)
    source = jnp.exp(0.5 * temps)
    layers = absorb[None, :] * source
    overhead = jnp.dot(layers, strict_upper, precision=PRECISE, preferred_element_type=jnp.float32)
    emitted = source * jnp.exp(-overhead) * -jnp.expm1(-layers)
    return jnp.dot(emitted, kernel, precision=PRECISE, preferred_element_type=jnp.float32)


def fourier_lookup(row_count, waves, points):
    orders = jnp.arange(waves, dtype=jnp.int32)
    places = jnp.arange(points, dtype=jnp.int32)
    phases = places[:, None] * orders[None, :] % row_count
    angles = 2.0 * math.pi * phases.astype(jnp.float32) / row_count.astype(jnp.float32)
    weights = jnp.where(orders == 0, 1.0, 2.0) * (2 * orders < row_count).astype(jnp.float32)
    return jnp.stack((weights * jnp.cos(angles), -weights * jnp.sin(angles)), axis=-1)


def synthesize_row(spectra, row_count, modes_basis, absorb, kernel, points):
    waves, hemis, columns = spectra.shape
    lookup = fourier_lookup(row_count, waves, points)
    split_parts = spectra.reshape(waves, hemis, 2, columns // 2)
    fields = jnp.einsum("kmq,mhqc->hkc", lookup, split_parts, precision=PRECISE)
    fields = jnp.einsum("hkc,cl->hkl", fields, modes_basis, precision=PRECISE)
    levels = fields.shape[-1]
    bright = radiate(fields.reshape(hemis * points, levels), absorb, kernel)
    bright = bright.reshape(hemis, points, kernel.shape[1])
    inside = (jnp.arange(points, dtype=jnp.int32) < row_count).astype(jnp.float32)
    return bright * inside[None, :, None]


def synthesize_rows(pieces, row_counts, modes_basis, absorb, kernel):
    results = [synthesize_row(pieces[:, :, 0, :], row_counts[0], modes_basis, absorb, kernel, NLON)]
    return jnp.stack(results, axis=0)


def legendre_rows(legendre, spectral):
    even_odd = jnp.einsum("mpsj,mpsc->mpjc", legendre, spectral, precision=PRECISE)
    return jnp.stack((even_odd[:, 0] + even_odd[:, 1], even_odd[:, 0] - even_odd[:, 1]), axis=1)


def on_device(coefficients, legendre, row_counts, basis, absorb, peak_level, width):
    first = lax.axis_index("spec") * coefficients.shape[2]
    scaled = prior_scale(coefficients, first)
    kernel = channel_kernel(peak_level, width, basis.shape[1])
    spectral = lax.all_to_all(scaled, "spec", split_axis=0, concat_axis=2, tiled=True)
    fourier = legendre_rows(legendre, spectral)
    return synthesize_rows(
        lax.all_to_all(fourier, "spec", split_axis=2, concat_axis=0, tiled=True),
        row_counts,
        basis,
        absorb,
        kernel,
    )


def solution(mesh):
    placed = (
        P("draws", None, "spec", None),
        P("spec", None, None, None),
        P("spec"),
        P(),
        P(),
        P(),
        P(),
    )
    return jax.shard_map(
        on_device,
        mesh=mesh,
        in_specs=placed,
        out_specs=P(("draws", "spec"), None, None, None),
        check_vma=False,
    )
```

profile of v0, /device:TPU:0, one launch (start us, length us, event | category | flops | bytes accessed | tf_op | source)
XLA Modules:
  0.0 469.3 jit_solution(60947047972407609)
XLA Ops:
  0.0 0.0 copy-start.1
  0.1 2.2 rsqrt_select_fusion
  2.3 0.8 copy-done.1
  3.0 16.7 %convert_multiply_fusion = f32[640,2,20,128]{3,1,2,0:T(2,128)} fusion(bf16[640,2,20,128]{3,1,2,0:T(2,128)(2,1)S(1)} %copy-done.1, f32[640,2,20]{1,2,0:T(8,128)S(1)} %rsqrt_select_fusion), kind=kLoop, calls=%fused_computation.2 | loop fusion | flops 6553600 | bytes 19763200 | tf_op jit(solution)/shard_map/mul | solution.py:23
  19.8 7.4 %all-to-all-start = ((f32[640,2,20,128]{3,1,2,0:T(2,128)}), f32[640,2,20,128]{3,1,2,0:T(2,128)}, u32[]{:S(2)}, u32[]{:S(2)}) async-start(f32[640,2,20,128]{3,1,2,0:T(2,128)} %convert_multiply_fusion), calls=%async_computation | async-start | bytes 26214400 | tf_op jit(solution)/shard_map/all_to_all | solution.py:79
  27.9 232.2 %all-to-all-done = f32[640,2,20,128]{3,1,2,0:T(2,128)} async-done(((f32[640,2,20,128]{3,1,2,0:T(2,128)}), f32[640,2,20,128]{3,1,2,0:T(2,128)}, u32[]{:S(2)}, u32[]{:S(2)}) %all-to-all-start) | async-done | bytes 13107232 | tf_op jit(solution)/shard_map/all_to_all | solution.py:79
  260.1 12.0 %copy.29 = f32[640,2,20,128]{3,0,2,1:T(8,128)} copy(f32[640,2,20,128]{3,1,2,0:T(2,128)} %all-to-all-done) | data formatting | bytes 26214400 | tf_op jit(solution)/shard_map/all_to_all | solution.py:79
  272.1 11.0 %copy.30 = f32[40,2,16,20,128]{4,0,3,2,1:T(8,128)} copy(f32[40,2,16,20,128]{4,0,2,3,1:T(8,128)} %bitcast.37) | data formatting | bytes 26214400 | tf_op jit(solution)/shard_map/all_to_all | solution.py:79
  283.1 13.6 %fusion.19 = f32[40,2,16,128]{3,2,1,0:T(8,128)S(1)} fusion(f32[40,2,320,16]{2,3,1,0:T(8,128)S(1)} %copy-done, f32[40,2,320,128]{3,0,2,1:T(8,128)} %bitcast.38), kind=kOutput, calls=%fused_computation.31 | convolution fusion | flops 629145600 | bytes 15400960 | tf_op jit(solution)/shard_map/mpsj,mpsc->mpjc/dot_general | solution.py:71
  296.9 0.0 copy-start.5
  296.9 0.0 copy-start.4
  296.9 1.2 copy.32
  298.1 55.6 %all-to-all-start.1 = ((f32[40,2,16,128]{3,1,0,2:T(2,128)}), f32[40,2,16,128]{3,1,0,2:T(2,128)S(1)}, u32[]{:S(2)}, u32[]{:S(2)}) async-start(f32[40,2,16,128]{3,1,0,2:T(2,128)} %copy.32), calls=%async_computation.1 | async-start | bytes 1310720 | tf_op jit(solution)/shard_map/all_to_all | solution.py:82
  353.7 43.5 %cosine_multiply_fusion = f32[1280,640,1]{1,0,2:T(8,128)} fusion(f32[640]{0:T(1024)S(1)} %get-tuple-element.7, f32[]{:T(128)S(6)} %convert_element_type.42, pred[]{:T(512)S(6)} %lt.70, s32[]{:T(128)S(6)} %select_n.41), kind=kLoop, calls=%fused_computation.19 | loop fusion | flops 9830400 | bytes 3279369 | tf_op jit(solution)/shard_map/mul | solution.py:49
  397.3 0.1 fusion.26
  397.4 43.8 %sine_multiply_fusion = f32[1280,640,1]{1,0,2:T(8,128)} fusion(f32[640]{0:T(1024)S(1)} %get-tuple-element.8, f32[]{:T(128)S(6)} %convert_element_type.42, pred[]{:T(512)S(6)} %lt.70, s32[]{:T(128)S(6)} %select_n.41), kind=kLoop, calls=%fused_computation.18 | loop fusion | flops 9830400 | bytes 3279369 | tf_op jit(solution)/shard_map/mul | solution.py:49
  441.2 0.8 copy-done.2
  442.0 2.3 reshape.184
  444.3 13.5 %fusion.17 = f32[2,1280,64]{1,2,0:T(8,128)S(1)} fusion(f32[1280,640,1]{1,0,2:T(8,128)} %sine_multiply_fusion, f32[1280,640,1]{1,0,2:T(8,128)} %cosine_multiply_fusion, f32[640,2,2,64]{3,2,1,0:T(2,128)S(1)} %reshape.184), kind=kOutput, calls=%fused_computation.28 | convolution fusion | flops 2518220800 | bytes 7864320 | tf_op jit(solution)/shard_map/kmq,mhqc->hkc/dot_general | solution.py:56
  457.9 2.5 fusion.16
  460.4 0.1 bitcast_multiply_fusion
  460.4 1.2 fusion.8
  461.6 4.5 fusion.23
  466.1 2.8 broadcast_multiply_fusion
  (17 shorter events, 0.2 us)
Async XLA Ops:
  0.0 283.1 %copy-start = (f32[40,2,320,16]{2,3,1,0:T(8,128)S(1)}, f32[40,2,320,16]{2,3,1,0:T(8,128)}, u32[]{:S(2)}) copy-start(f32[40,2,320,16]{2,3,1,0:T(8,128)} %param.8) | copy-start | bytes 4915204
  0.0 3.0 copy-start.1
  19.8 240.3 %all-to-all-start = ((f32[640,2,20,128]{3,1,2,0:T(2,128)}), f32[640,2,20,128]{3,1,2,0:T(2,128)}, u32[]{:S(2)}, u32[]{:S(2)}) async-start(f32[640,2,20,128]{3,1,2,0:T(2,128)} %convert_multiply_fusion), calls=%async_computation | async-start | bytes 26214400 | tf_op jit(solution)/shard_map/all_to_all | solution.py:79
  296.9 100.4 %copy-start.5 = (s32[512]{0:T(512)S(1)}, s32[512]{0:T(512)}, u32[]{:S(2)}) copy-start(s32[512]{0:T(512)} %param.12) | copy-start | bytes 6148
  296.9 100.4 %copy-start.4 = (f32[512]{0:T(512)S(1)}, f32[512]{0:T(512)}, u32[]{:S(2)}) copy-start(f32[512]{0:T(512)} %param.13) | copy-start | bytes 6148
  298.1 143.1 %all-to-all-start.1 = ((f32[40,2,16,128]{3,1,0,2:T(2,128)}), f32[40,2,16,128]{3,1,0,2:T(2,128)S(1)}, u32[]{:S(2)}, u32[]{:S(2)}) async-start(f32[40,2,16,128]{3,1,0,2:T(2,128)} %copy.32), calls=%async_computation.1 | async-start | bytes 1310720 | tf_op jit(solution)/shard_map/all_to_all | solution.py:82
  441.2 0.8 copy-start.2
  444.3 13.5 %copy-start.3 = (f32[64,128]{1,0:T(8,128)S(1)}, f32[64,128]{1,0:T(8,128)}, u32[]{:S(2)}) copy-start(f32[64,128]{1,0:T(8,128)} %param.10) | copy-start | bytes 98308
  444.3 16.0 %copy-start.6 = (f32[128]{0:T(128)S(1)}, f32[128]{0:T(128)}, u32[]{:S(2)}) copy-start(f32[128]{0:T(128)} %param.11) | copy-start | bytes 1540
where the time goes:
time: 478 us; the launch traced here: 469 us
  waiting for transfers between devices  232 us (49%)
  other arithmetic  109 us (23%)
  starting transfers between devices  63.1 us (13%)
  matrix products  35.3 us (7%)
  local copies, waits for them, and re-layouts  28.1 us (6%)
    all_to_all x1, waiting for transfers between devices, on_device(): lax.all_to_all(scaled, 'spec', split_axis=0, concat_axis=2, tiled=True)  232 us
    all_to_all x1, starting transfers between devices, on_device(): lax.all_to_all(fourier, 'spec', split_axis=2, concat_axis=0, tiled=True)  55.6 us
    mul x1, other arithmetic, fourier_lookup(): -weights * jnp.sin(angles)  43.8 us
    mul x1, other arithmetic, fourier_lookup(): weights * jnp.cos(angles)  43.5 us
    all_to_all x2, local copies, waits for them, and re-layouts, on_device(): lax.all_to_all(scaled, 'spec', split_axis=0, concat_axis=2, tiled=True)  23 us
    mul x1, other arithmetic, prior_scale(): return shard.astype(jnp.float32) * spread[..., None]  16.7 us
    dot_general x1, matrix products, legendre_rows(): jnp.einsum('mpsj,mpsc->mpjc', legendre, spectral, precision=PRECISE)  13.6 us
    dot_general x1, matrix products, synthesize_row(): fields = jnp.einsum('kmq,mhqc->hkc', lookup, split_parts, precision=PRECISE)  13.5 us
  transfers between devices with their start and end apart: 2, of which 1 were waited for; matrix products, arithmetic and copies ran while one was open for 19% of the time, Pallas kernels for 0%

commit v1 on v0

v1 whole, which is shorter than its diff:
```python
import functools
import math

import jax
import jax.numpy as jnp
from jax import lax
from jax.experimental import pallas as pl
from jax.experimental.pallas import tpu as pltpu
from jax.sharding import PartitionSpec as P

NLON = 1280
STEP = 32
PLANES = 4
PAD = 32

PRECISE = lax.Precision.HIGHEST
F32 = jnp.float32
BF16 = jnp.bfloat16


def prior_scale(shard, first):
    waves = shard.shape[0]
    slots = shard.shape[2]
    orders = jnp.arange(waves, dtype=jnp.int32)[:, None, None]
    parity = jnp.arange(2, dtype=jnp.int32)[None, :, None]
    slot_index = first + jnp.arange(slots, dtype=jnp.int32)[None, None, :]
    degree = orders + 2 * slot_index + parity
    spread = lax.rsqrt((degree + 1).astype(F32) * waves)
    spread = jnp.where(degree < waves, spread, jnp.zeros_like(spread))
    return shard.astype(F32) * spread[..., None]


def channel_kernel(peak_level, width, levels):
    height = jnp.arange(levels, dtype=F32)[:, None]
    offsets = (height - peak_level.astype(F32)[None, :]) / width[None, :]
    weights = jnp.exp(-offsets * offsets)
    return weights / jnp.sum(weights, axis=0, keepdims=True)


def radiate(temps, absorb, kernel):
    levels = temps.shape[-1]
    strict_upper = (jnp.arange(levels)[:, None] < jnp.arange(levels)[None, :]).astype(F32)
    source = jnp.exp(0.5 * temps)
    layers = absorb[None, :] * source
    overhead = jnp.dot(layers, strict_upper, precision=PRECISE, preferred_element_type=F32)
    emitted = source * jnp.exp(-overhead) * -jnp.expm1(-layers)
    return jnp.dot(emitted, kernel, precision=PRECISE, preferred_element_type=F32)


def fourier_lookup(row_count, waves, points):
    orders = jnp.arange(waves, dtype=jnp.int32)
    places = jnp.arange(points, dtype=jnp.int32)
    phases = places[:, None] * orders[None, :] % row_count
    angles = 2.0 * math.pi * phases.astype(F32) / row_count.astype(F32)
    weights = jnp.where(orders == 0, 1.0, 2.0) * (2 * orders < row_count).astype(F32)
    return jnp.stack((weights * jnp.cos(angles), -weights * jnp.sin(angles)), axis=-1)


def synthesize_row(spectra, row_count, modes_basis, absorb, kernel, points):
    waves, hemis, columns = spectra.shape
    lookup = fourier_lookup(row_count, waves, points)
    split_parts = spectra.reshape(waves, hemis, 2, columns // 2)
    fields = jnp.einsum("kmq,mhqc->hkc", lookup, split_parts, precision=PRECISE)
    fields = jnp.einsum("hkc,cl->hkl", fields, modes_basis, precision=PRECISE)
    levels = fields.shape[-1]
    bright = radiate(fields.reshape(hemis * points, levels), absorb, kernel)
    bright = bright.reshape(hemis, points, kernel.shape[1])
    inside = (jnp.arange(points, dtype=jnp.int32) < row_count).astype(F32)
    return bright * inside[None, :, None]


def legendre_rows(legendre, spectral):
    even_odd = jnp.einsum("mpsj,mpsc->mpjc", legendre, spectral, precision=PRECISE)
    return jnp.stack((even_odd[:, 0] + even_odd[:, 1], even_odd[:, 0] - even_odd[:, 1]), axis=1)


def move_coefficients(coefficients, legendre, row_counts, basis, absorb, peak_level, width):
    first = lax.axis_index("spec") * coefficients.shape[2]
    scaled = prior_scale(coefficients, first)
    kernel = channel_kernel(peak_level, width, basis.shape[1])
    spectral = lax.all_to_all(scaled, "spec", split_axis=0, concat_axis=2, tiled=True)
    fourier = legendre_rows(legendre, spectral)
    pieces = lax.all_to_all(fourier, "spec", split_axis=2, concat_axis=0, tiled=True)
    row = synthesize_row(pieces[:, :, 0, :], row_counts[0], basis, absorb, kernel, NLON)
    return row[None]


def split_pair(value):
    high = value.astype(BF16)
    return high, (value - high.astype(F32)).astype(BF16)


def split_constant(value):
    high = lax.reduce_precision(value, exponent_bits=8, mantissa_bits=7)
    return high.astype(BF16), (value - high).astype(BF16)


def arrange_legendre(legendre, first_wave, spec, waves):
    held, _, slots, rows = legendre.shape
    groups, own = held // 4, slots // spec
    lanes = rows * 8

    def body(first_ref, leg_ref, out_ref, turned):
        pair = lax.broadcasted_iota(jnp.int32, (8, slots), 0)
        slot = lax.broadcasted_iota(jnp.int32, (8, slots), 1)
        for group in range(groups):
            degree = first_ref[0] + 4 * group + pair // 2 + 2 * slot + pair % 2
            spread = lax.rsqrt((degree + 1).astype(F32) * waves)
            spread = jnp.where(degree < waves, spread, 0.0)
            block = leg_ref[4 * group:4 * group + 4].reshape(8, rows, slots)
            block = block * spread[:, None, :]
            block = jnp.swapaxes(block, 0, 1).reshape(lanes, slots)
            turned[...] = block.T
            for goal in range(spec):
                out_ref[goal, group * own:(group + 1) * own, :] = turned[goal * own:(goal + 1) * own, :]

    return pl.pallas_call(
        body,
        grid_spec=pltpu.PrefetchScalarGridSpec(
            num_scalar_prefetch=1,
            grid=(1,),
            in_specs=[pl.BlockSpec((held, 2, rows, slots), lambda i, f: (0, 0, 0, 0))],
            out_specs=pl.BlockSpec((spec, groups * own, lanes), lambda i, f: (0, 0, 0)),
            scratch_shapes=[pltpu.VMEM((slots, lanes), F32)],
        ),
        out_shape=jax.ShapeDtypeStruct((spec, groups * own, lanes), F32),
        compiler_params=pltpu.CompilerParams(vmem_limit_bytes=32 << 20),
        cost_estimate=pl.CostEstimate(flops=4_000_000, bytes_accessed=4_000_000, transcendentals=0),
        name="arrange_legendre",
    )(first_wave, jnp.transpose(legendre, (0, 1, 3, 2)))


def partial_rows(order, arranged, padded, sources, own):
    spec, depth, lanes = arranged.shape
    groups = depth // own
    rows = lanes // 8
    half = rows // 2
    columns = padded.shape[-1]

    def body(order_ref, leg_ref, coef_ref, keep_ref, send_ref, spread_ref):
        spread_ref[...] = jnp.zeros_like(spread_ref)
        row = lax.broadcasted_iota(jnp.int32, (lanes, 4 * PAD), 0) % 8
        block = lax.broadcasted_iota(jnp.int32, (lanes, 4 * PAD), 1) // PAD
        here = [row == block, row == block + 4]
        first_core = jnp.full((8, columns), order_ref[3 * sources + half], jnp.int32) == 0
        for group in range(groups):
            piece = leg_ref[0, group * own:(group + 1) * own, :]
            for copy in range(4):
                spread_ref[copy * PAD:copy * PAD + own, :] = piece
            turned = spread_ref[...].T
            parts = [split_pair(jnp.where(mask, turned, 0.0)) for mask in here]
            high = jnp.concatenate([parts[0][0], parts[1][0]], axis=1)
            low = jnp.concatenate([parts[0][1], parts[1][1]], axis=1)
            coef = coef_ref[group]
            total = jnp.dot(high, coef, preferred_element_type=F32) + jnp.dot(low, coef, preferred_element_type=F32)
            for couple in range(half):
                one = total[16 * couple:16 * couple + 8]
                two = total[16 * couple + 8:16 * couple + 16]
                place = order_ref[3 * sources + couple]
                keep_ref[place, 8 * group:8 * group + 8, :] = jnp.where(first_core, one, two)
                send_ref[place, 8 * group:8 * group + 8, :] = jnp.where(first_core, two, one)

    out = jax.ShapeDtypeStruct((half, sources * groups * 8, columns), F32)
    out_spec = pl.BlockSpec((half, groups * 8, columns), lambda i, o: (0, o[2 * sources + i], 0))
    return pl.pallas_call(
        body,
        grid_spec=pltpu.PrefetchScalarGridSpec(
            num_scalar_prefetch=1,
            grid=(sources,),
            in_specs=[
                pl.BlockSpec((1, depth, lanes), lambda i, o: (o[i], 0, 0)),
                pl.BlockSpec((groups, 8 * PAD, columns), lambda i, o: (o[sources + i], 0, 0)),
            ],
            out_specs=[out_spec, out_spec],
            scratch_shapes=[pltpu.VMEM((4 * PAD, lanes), F32)],
        ),
        out_shape=[out, out],
        compiler_params=pltpu.CompilerParams(vmem_limit_bytes=32 << 20),
        cost_estimate=pl.CostEstimate(flops=500_000_000, bytes_accessed=6_000_000, transcendentals=0),
        name="partial_rows",
    )(order, arranged, padded)


def wave_tables(row_count, waves):
    orders = jnp.arange(waves, dtype=jnp.int32)
    weights = jnp.where(orders == 0, 1.0, 2.0) * (2 * orders < row_count).astype(F32)
    coarse = STEP * jnp.arange(NLON // STEP, dtype=jnp.int32)
    places = jnp.concatenate((coarse, jnp.arange(STEP, dtype=jnp.int32)))
    phases = places[:, None] * orders[None, :] % row_count
    angles = 2.0 * math.pi * phases.astype(F32) / row_count.astype(F32)
    gain = jnp.where(jnp.arange(places.shape[0])[:, None] < coarse.shape[0], weights[None, :], 1.0)
    return gain * jnp.cos(angles), gain * jnp.sin(angles)


def synthesize(row_counts, spectra, tables, basis, absorb, kernel):
    waves = spectra.shape[0] // 2
    columns = spectra.shape[1]
    levels = basis.shape[1]
    modes = basis.shape[0]
    channels = kernel.shape[1]
    coarse = NLON // STEP
    tile = 4 * STEP
    zero = jnp.zeros_like(basis)
    widened = jnp.concatenate((basis, zero, zero, -basis), axis=0)
    basis_high, basis_low = split_constant(widened)
    kernel_high, kernel_low = split_constant(kernel)

    def body(count_ref, spec_ref, cos_ref, sin_ref, bh_ref, bl_ref, ab_ref, kh_ref, kl_ref, out_ref, high_ref, low_ref):
        step = pl.program_id(0)

        @pl.when(step == 0)
        def _():
            for parity in range(2):
                value = spec_ref[pl.ds(parity, waves, stride=2), :]
                high, low = split_pair(value)
                high_ref[:, parity * columns:(parity + 1) * columns] = high
                low_ref[:, parity * columns:(parity + 1) * columns] = low

        cos_fine, sin_fine = cos_ref[coarse:, :], sin_ref[coarse:, :]
        cosines, sines = [], []
        for part in range(tile // STEP):
            at = step * (tile // STEP) + part
            cos_at, sin_at = cos_ref[pl.ds(at, 1), :], sin_ref[pl.ds(at, 1), :]
            cosines.append(cos_at * cos_fine - sin_at * sin_fine)
            sines.append(sin_at * cos_fine + cos_at * sin_fine)
        high, low = split_pair(jnp.concatenate(cosines + sines, axis=0))
        fields = jnp.dot(high, high_ref[...], preferred_element_type=F32)
        fields += jnp.dot(low, high_ref[...], preferred_element_type=F32)
        fields += jnp.dot(high, low_ref[...], preferred_element_type=F32)
        even, odd = fields[:, :columns], fields[:, columns:]
        north, south = even + odd, even - odd
        both = jnp.concatenate(
            [jnp.concatenate([side[:tile], side[tile:]], axis=1) for side in (north, south)], axis=0
        )
        high, low = split_pair(both)
        temps = jnp.dot(high, bh_ref[...], preferred_element_type=F32)
        temps += jnp.dot(low, bh_ref[...], preferred_element_type=F32)
        temps += jnp.dot(high, bl_ref[...], preferred_element_type=F32)
        source = jnp.exp(0.5 * temps)
        layers = ab_ref[...] * source
        above = lax.broadcasted_iota(jnp.int32, (2 * levels, levels), 0) % levels
        level = lax.broadcasted_iota(jnp.int32, (2 * levels, levels), 1)
        upper = jnp.where(above < level, 1.0, 0.0).astype(BF16)
        overhead = jnp.dot(jnp.concatenate(split_pair(layers), axis=1), upper, preferred_element_type=F32)
        half = jnp.tanh(0.5 * layers)
        emitted = source * jnp.exp(-overhead) * (2.0 * half / (1.0 + half))
        high, low = split_pair(emitted)
        bright = jnp.dot(high, kh_ref[...], preferred_element_type=F32)
        bright += jnp.dot(low, kh_ref[...], preferred_element_type=F32)
        bright += jnp.dot(high, kl_ref[...], preferred_element_type=F32)
        place = step * tile + lax.broadcasted_iota(jnp.int32, (2 * tile, 1), 0) % tile
        bright = jnp.where(place < count_ref[0], bright, 0.0)
        out_ref[0] = bright.reshape(2, tile, channels)

    def whole(array):
        return pl.BlockSpec(array.shape, lambda i, c: (0,) * array.ndim)

    operands = (spectra, *tables, basis_high, basis_low, absorb[None, :], kernel_high, kernel_low)
    return pl.pallas_call(
        body,
        grid_spec=pltpu.PrefetchScalarGridSpec(
            num_scalar_prefetch=1,
            grid=(NLON // tile,),
            in_specs=[whole(array) for array in operands],
            out_specs=pl.BlockSpec((1, 2, tile, channels), lambda i, c: (0, 0, i, 0)),
            scratch_shapes=[pltpu.VMEM((waves, 2 * columns), BF16)] * 2,
        ),
        out_shape=jax.ShapeDtypeStruct((1, 2, NLON, channels), F32),
        compiler_params=pltpu.CompilerParams(vmem_limit_bytes=48 << 20),
        cost_estimate=pl.CostEstimate(flops=4_000_000_000, bytes_accessed=8_000_000, transcendentals=2_000_000),
        name="synthesize",
    )(row_counts, *operands)


def move_legendre(spec, coefficients, legendre, row_counts, basis, absorb, peak_level, width):
    waves, _, own, columns = coefficients.shape
    held = legendre.shape[0]
    groups = held // 4
    me = lax.axis_index("spec").astype(jnp.int32)
    arranged = arrange_legendre(legendre, (me * held)[None], spec, waves)
    arrived = lax.all_to_all(arranged, "spec", split_axis=0, concat_axis=0, tiled=True)
    padded = jnp.pad(coefficients, ((0, 0), (0, 0), (0, PAD - own), (0, 0)))
    padded = padded.reshape(waves // 4, 8 * PAD, columns)
    tables = wave_tables(row_counts[0], waves)
    kernel = channel_kernel(peak_level, width, basis.shape[1])

    def swap(value, distance):
        return lax.ppermute(value, "spec", [(i, i ^ distance) for i in range(spec)])

    sources = spec // PLANES
    couple = jnp.arange(spec // 2, dtype=jnp.int32) ^ (me >> 1)
    place = (couple & 1) * (spec // 4) + (couple >> 1)
    pieces = []
    for plane in range(PLANES):
        local = jnp.arange(sources, dtype=jnp.int32)
        source = plane * sources + local
        order = jnp.concatenate((source, source, local, place, (me & 1)[None]))
        keep, send = partial_rows(order, arrived, padded, sources, own)
        other = swap(send, 1)
        quarter = spec // 4
        send, keep = keep[quarter:] + other[quarter:], keep[:quarter] + other[:quarter]
        both = keep + swap(send, 2)
        total = both[0]
        for away in range(1, quarter):
            total = total + swap(both[away], 4 * away)
        pieces.append(total)
    spectra = jnp.concatenate(pieces, axis=0)
    return synthesize(row_counts, spectra, tables, basis, absorb, kernel)


def solution(mesh):
    spec = mesh.shape["spec"]
    placed = (
        P("draws", None, "spec", None),
        P("spec", None, None, None),
        P("spec"),
        P(),
        P(),
        P(),
        P(),
    )

    def on_device(coefficients, legendre, *others):
        held, _, _, rows = legendre.shape
        own = coefficients.shape[2]
        small = rows == spec and 8 * rows == 4 * PAD and held % 4 == 0 and rows <= own <= PAD
        if small:
            return move_legendre(spec, coefficients, legendre, *others)
        return move_coefficients(coefficients, legendre, *others)

    return jax.shard_map(
        on_device,
        mesh=mesh,
        in_specs=placed,
        out_specs=P(("draws", "spec"), None, None, None),
        check_vma=False,
    )
```

time: 478 us -> 197 us (0.41); the launches traced: 469 us -> 196 us
  waiting for transfers between devices: 232 us -> 70.7 us
  other arithmetic: 109 us -> 13 us
  Pallas kernels: 0 us -> 35.4 us
  matrix products: 35.3 us -> 0 us
  starting transfers between devices: 63.1 us -> 50.1 us
    all_to_all x2 -> x1, waiting for transfers between devices: 232 us -> 14.6 us  [move_legendre(): lax.all_to_all(arranged, 'spec', split_axis=0, concat_axis=0, tiled=True)]
    mul x7 -> x3, other arithmetic: 107 us -> 2.57 us  [the longest x1 2.56 us: wave_tables(): return (gain * jnp.cos(angles), gain * jnp.sin(angles))]
    ppermute x0 -> x20, waiting for transfers between devices: none -> 56.1 us  [swap(): return lax.ppermute(value, 'spec', [(i, i ^ distance) for i in range(spec)])]
    all_to_all x2 -> x1, starting transfers between devices: 63.1 us -> 7.39 us  [move_legendre(): lax.all_to_all(arranged, 'spec', split_axis=0, concat_axis=0, tiled=True)]
    ppermute x0 -> x20, starting transfers between devices: none -> 42.8 us  [swap(): return lax.ppermute(value, 'spec', [(i, i ^ distance) for i in range(spec)])]
    pallas_call x0 -> x6, Pallas kernels: none -> 35.4 us  [the longest x1 17.7 us: synthesize(): pl.pallas_call(body, grid_spec=pltpu.PrefetchScalarGridSpec(num_scalar_pr...]
    dot_general x5 -> x0, matrix products: 35.3 us -> none  [the longest x1 13.6 us: legendre_rows(): jnp.einsum('mpsj,mpsc->mpjc', legendre, spectral, precision=PRECISE)]
    all_to_all x2 -> x0, local copies, waits for them, and re-layouts: 23 us -> none  [on_device(): lax.all_to_all(scaled, 'spec', split_axis=0, concat_axis=2, tiled=True)]
  transfers between devices with their start and end apart: 2 -> 21, of which waited for: 1 -> 8; matrix products, arithmetic and copies ran while one was open for 19% -> 16% of each run, Pallas kernels for 0% -> 6%
where the time goes in v1:
time: 197 us; the launch traced here: 196 us
  waiting for transfers between devices  70.7 us (36%)
  starting transfers between devices  50.1 us (25%)
  Pallas kernels  35.4 us (18%)
  local copies, waits for them, and re-layouts  25.7 us (13%)
  other arithmetic  13 us (7%)
    ppermute x20, waiting for transfers between devices, swap(): return lax.ppermute(value, 'spec', [(i, i ^ distance) for i in range(spec)])  56.1 us
    ppermute x20, starting transfers between devices, swap(): return lax.ppermute(value, 'spec', [(i, i ^ distance) for i in range(spec)])  42.8 us
    pallas_call x1, Pallas kernels, synthesize(): pl.pallas_call(body, grid_spec=pltpu.PrefetchScalarGridSpec(num_scalar_pr...  17.7 us
    pallas_call x4, Pallas kernels, partial_rows(): pl.pallas_call(body, grid_spec=pltpu.PrefetchScalarGridSpec(num_scalar_pr...  15.7 us
    unnamed x31, local copies, waits for them, and re-layouts  14.9 us
    all_to_all x1, waiting for transfers between devices, move_legendre(): lax.all_to_all(arranged, 'spec', split_axis=0, concat_axis=0, tiled=True)  14.6 us
    pad x1, local copies, waits for them, and re-layouts, move_legendre(): padded = jnp.pad(coefficients, ((0, 0), (0, 0), (0, PAD - own), (0, 0)))  10.2 us
    all_to_all x1, starting transfers between devices, move_legendre(): lax.all_to_all(arranged, 'spec', split_axis=0, concat_axis=0, tiled=True)  7.39 us
  transfers between devices with their start and end apart: 21, of which 8 were waited for; matrix products, arithmetic and copies ran while one was open for 16% of the time, Pallas kernels for 6%

profile of v1, /device:TPU:0, one launch (start us, length us, event | category | flops | bytes accessed | tf_op | source)
XLA Modules:
  0.0 195.9 jit_solution(17209864461413056570)
XLA Ops:
  3.5 7.4 %all-to-all-start = ((f32[16,200,128]{2,1,0:T(8,128)}), f32[16,200,128]{2,1,0:T(8,128)S(1)}, u32[]{:S(2)}, u32[]{:S(2)}) async-start(f32[16,200,128]{2,1,0:T(8,128)} %arrange_legendre.1), calls=%async_computation | async-start | bytes 3276800 | tf_op jit(solution)/shard_map/all_to_all | solution.py:281
  11.0 7.2 %copy.9 = bf16[640,2,20,128]{3,2,1,0:T(8,128)(2,1)} copy(bf16[640,2,20,128]{3,1,2,0:T(2,128)(2,1)} %param.7) | data formatting | bytes 13107200
  18.8 10.2 %pad.4.clone = bf16[640,2,32,128]{3,2,1,0:T(8,128)(2,1)} pad(bf16[640,2,20,128]{3,2,1,0:T(8,128)(2,1)} %copy.9, bf16[]{:T(256)} %constant.18.clone.1), padding=0_0x0_0x0_12x0_0 | pad | bytes 17039362 | tf_op jit(solution)/shard_map/jit(_pad)/pad | solution.py:282
  29.5 14.6 %all-to-all-done.leg_ref = f32[16,200,128]{2,1,0:T(8,128)S(1)} async-done(((f32[16,200,128]{2,1,0:T(8,128)}), f32[16,200,128]{2,1,0:T(8,128)S(1)}, u32[]{:S(2)}, u32[]{:S(2)}) %all-to-all-start) | async-done | bytes 1638432 | tf_op jit(solution)/shard_map/all_to_all | solution.py:281
  44.0 4.0 %copy-done = bf16[640,2,32,128]{3,2,1,0:T(8,128)(2,1)S(1)} copy-done((bf16[640,2,32,128]{3,2,1,0:T(8,128)(2,1)S(1)}, bf16[640,2,32,128]{3,2,1,0:T(8,128)(2,1)}, u32[]{:S(2)}) %copy-start) | copy-done | bytes 10485784
  48.0 4.0 %partial_rows.4 = (f32[8,320,128]{2,1,0:T(8,128)S(1)}, f32[8,320,128]{2,1,0:T(8,128)}) custom-call(s32[21]{0:T(128)S(1)} %concatenate.24.order_ref, f32[16,200,128]{2,1,0:T(8,128)S(1)} %all-to-all-done.leg_ref, bf16[160,256,128]{2,1,0:T(8,128)(2,1)S(1)} %bitcast.66), custom_call_target="tpu_custom_call" | custom-call | flops 500000000 | bytes 6000000 | tf_op jit(solution)/shard_map/partial_rows/pallas_call | solution.py:165
  53.9 3.9 %partial_rows.5 = (f32[8,320,128]{2,1,0:T(8,128)S(1)}, f32[8,320,128]{2,1,0:T(8,128)}) custom-call(s32[21]{0:T(128)S(1)} %concatenate.25.order_ref, f32[16,200,128]{2,1,0:T(8,128)S(1)} %all-to-all-done.leg_ref, bf16[160,256,128]{2,1,0:T(8,128)(2,1)S(1)} %bitcast.67), custom_call_target="tpu_custom_call" | custom-call | flops 500000000 | bytes 6000000 | tf_op jit(solution)/shard_map/partial_rows/pallas_call | solution.py:165
  59.1 3.9 %partial_rows.6 = (f32[8,320,128]{2,1,0:T(8,128)S(1)}, f32[8,320,128]{2,1,0:T(8,128)}) custom-call(s32[21]{0:T(128)S(1)} %concatenate.26.order_ref, f32[16,200,128]{2,1,0:T(8,128)S(1)} %all-to-all-done.leg_ref, bf16[160,256,128]{2,1,0:T(8,128)(2,1)S(1)} %bitcast.68), custom_call_target="tpu_custom_call" | custom-call | flops 500000000 | bytes 6000000 | tf_op jit(solution)/shard_map/partial_rows/pallas_call | solution.py:165
  63.6 3.9 %partial_rows.7 = (f32[8,320,128]{2,1,0:T(8,128)S(1)}, f32[8,320,128]{2,1,0:T(8,128)}) custom-call(s32[21]{0:T(128)S(1)} %concatenate.27.order_ref, f32[16,200,128]{2,1,0:T(8,128)S(1)} %all-to-all-done.leg_ref, bf16[160,256,128]{2,1,0:T(8,128)(2,1)S(1)} %bitcast.71), custom_call_target="tpu_custom_call" | custom-call | flops 500000000 | bytes 6000000 | tf_op jit(solution)/shard_map/partial_rows/pallas_call | solution.py:165
  71.7 2.8 %collective-permute-start.1 = (f32[4,320,128]{2,1,0:T(8,128)S(1)}, f32[4,320,128]{2,1,0:T(8,128)S(1)}, u32[]{:S(2)}, u32[]{:S(2)}) collective-permute-start(f32[4,320,128]{2,1,0:T(8,128)S(1)} %slice_add_fusion.6), channel_id=1, source_target_pairs={{0,2},{1,3},{2,0},{3,1},{4,6},{5,7},{6,4},{7,5},{8,10},{9,11},{10,... | collective-permute-start | bytes 1966088 | tf_op jit(solution)/shard_map/ppermute | solution.py:288
  80.4 9.7 %collective-permute-done.1 = f32[4,320,128]{2,1,0:T(8,128)S(1)} collective-permute-done((f32[4,320,128]{2,1,0:T(8,128)S(1)}, f32[4,320,128]{2,1,0:T(8,128)S(1)}, u32[]{:S(2)}, u32[]{:S(2)}) %collective-permute-start.1) | collective-permute-done | bytes 655392 | tf_op jit(solution)/shard_map/ppermute | solution.py:288
  91.4 4.7 %collective-permute-start.2 = (f32[320,128]{1,0:T(8,128)S(1)}, f32[320,128]{1,0:T(8,128)S(1)}, u32[]{:S(2)}, u32[]{:S(2)}) collective-permute-start(f32[320,128]{1,0:T(8,128)S(1)} %get-tuple-element.21), channel_id=1, source_target_pairs={{0,4},{1,5},{2,6},{3,7},{4,0},{5,1},{6,2},{7,3},{8,12},{9,13},{10,... | collective-permute-start | bytes 491528 | tf_op jit(solution)/shard_map/ppermute | solution.py:288
  98.0 6.1 %collective-permute-done.6 = f32[4,320,128]{2,1,0:T(8,128)S(1)} collective-permute-done((f32[4,320,128]{2,1,0:T(8,128)S(1)}, f32[4,320,128]{2,1,0:T(8,128)S(1)}, u32[]{:S(2)}, u32[]{:S(2)}) %collective-permute-start.6) | collective-permute-done | bytes 655392 | tf_op jit(solution)/shard_map/ppermute | solution.py:288
  104.1 5.5 %collective-permute-start.4 = (f32[320,128]{1,0:T(8,128)S(1)}, f32[320,128]{1,0:T(8,128)S(1)}, u32[]{:S(2)}, u32[]{:S(2)}) collective-permute-start(f32[320,128]{1,0:T(8,128)S(1)} %get-tuple-element.22), channel_id=1, source_target_pairs={{0,12},{1,13},{2,14},{3,15},{4,8},{5,9},{6,10},{7,11},{8,4},{9,5},... | collective-permute-start | bytes 491528 | tf_op jit(solution)/shard_map/ppermute | solution.py:288
  110.9 7.3 %collective-permute-done.11 = f32[4,320,128]{2,1,0:T(8,128)S(1)} collective-permute-done((f32[4,320,128]{2,1,0:T(8,128)S(1)}, f32[4,320,128]{2,1,0:T(8,128)S(1)}, u32[]{:S(2)}, u32[]{:S(2)}) %collective-permute-start.11) | collective-permute-done | bytes 655392 | tf_op jit(solution)/shard_map/ppermute | solution.py:288
  118.2 4.6 %collective-permute-start.7 = (f32[320,128]{1,0:T(8,128)S(1)}, f32[320,128]{1,0:T(8,128)S(1)}, u32[]{:S(2)}, u32[]{:S(2)}) collective-permute-start(f32[320,128]{1,0:T(8,128)S(1)} %get-tuple-element.24), channel_id=1, source_target_pairs={{0,4},{1,5},{2,6},{3,7},{4,0},{5,1},{6,2},{7,3},{8,12},{9,13},{10,... | collective-permute-start | bytes 491528 | tf_op jit(solution)/shard_map/ppermute | solution.py:288
  124.1 8.0 %collective-permute-done.16 = f32[4,320,128]{2,1,0:T(8,128)S(1)} collective-permute-done((f32[4,320,128]{2,1,0:T(8,128)S(1)}, f32[4,320,128]{2,1,0:T(8,128)S(1)}, u32[]{:S(2)}, u32[]{:S(2)}) %collective-permute-start.16) | collective-permute-done | bytes 655392 | tf_op jit(solution)/shard_map/ppermute | solution.py:288
  132.0 5.8 %collective-permute-start.8 = (f32[320,128]{1,0:T(8,128)S(1)}, f32[320,128]{1,0:T(8,128)S(1)}, u32[]{:S(2)}, u32[]{:S(2)}) collective-permute-start(f32[320,128]{1,0:T(8,128)S(1)} %get-tuple-element.26), channel_id=1, source_target_pairs={{0,8},{1,9},{2,10},{3,11},{4,12},{5,13},{6,14},{7,15},{8,0},{9,1},... | collective-permute-start | bytes 491528 | tf_op jit(solution)/shard_map/ppermute | solution.py:288
  140.3 3.3 %collective-permute-start.13 = (f32[320,128]{1,0:T(8,128)S(1)}, f32[320,128]{1,0:T(8,128)S(1)}, u32[]{:S(2)}, u32[]{:S(2)}) collective-permute-start(f32[320,128]{1,0:T(8,128)S(1)} %get-tuple-element.29), channel_id=1, source_target_pairs={{0,8},{1,9},{2,10},{3,11},{4,12},{5,13},{6,14},{7,15},{8,0},{9,1},... | collective-permute-start | bytes 491528 | tf_op jit(solution)/shard_map/ppermute | solution.py:288
  144.8 10.6 %collective-permute-done.8 = f32[320,128]{1,0:T(8,128)S(1)} collective-permute-done((f32[320,128]{1,0:T(8,128)S(1)}, f32[320,128]{1,0:T(8,128)S(1)}, u32[]{:S(2)}, u32[]{:S(2)}) %collective-permute-start.8) | collective-permute-done | bytes 163872 | tf_op jit(solution)/shard_map/ppermute | solution.py:288
  155.4 6.3 %collective-permute-start.18 = (f32[320,128]{1,0:T(8,128)S(1)}, f32[320,128]{1,0:T(8,128)S(1)}, u32[]{:S(2)}, u32[]{:S(2)}) collective-permute-start(f32[320,128]{1,0:T(8,128)S(1)} %get-tuple-element.32), channel_id=1, source_target_pairs={{0,8},{1,9},{2,10},{3,11},{4,12},{5,13},{6,14},{7,15},{8,0},{9,1},... | collective-permute-start | bytes 491528 | tf_op jit(solution)/shard_map/ppermute | solution.py:288
  163.6 7.5 %collective-permute-done.13 = f32[320,128]{1,0:T(8,128)S(1)} collective-permute-done((f32[320,128]{1,0:T(8,128)S(1)}, f32[320,128]{1,0:T(8,128)S(1)}, u32[]{:S(2)}, u32[]{:S(2)}) %collective-permute-start.13) | collective-permute-done | bytes 163872 | tf_op jit(solution)/shard_map/ppermute | solution.py:288
  171.1 7.0 %collective-permute-done.18 = f32[320,128]{1,0:T(8,128)S(1)} collective-permute-done((f32[320,128]{1,0:T(8,128)S(1)}, f32[320,128]{1,0:T(8,128)S(1)}, u32[]{:S(2)}, u32[]{:S(2)}) %collective-permute-start.18) | collective-permute-done | bytes 163872 | tf_op jit(solution)/shard_map/ppermute | solution.py:288
  178.2 17.7 %synthesize.1 = f32[1,2,1280,512]{3,2,1,0:T(8,128)} custom-call(s32[1]{0:T(128)} %copy.10.count_ref, f32[1280,128]{1,0:T(8,128)S(1)} %pad_maximum_fusion.spec_ref, f32[72,640]{1,0:T(8,128)S(1)} %get-tuple-element.38.cos_ref, f32[72,640]{1,0:T(8,128)S(1)} %get-tuple-element.37.sin_ref, bf16[256,128]{1,0:T(8,128)(2,1)S(1)} %get-tuple-element.34.bh_ref, ...), custom_call_target="tpu_custom_call" | custom-call | flops 4000000000 | bytes 8000000 | tf_op jit(solution)/shard_map/synthesize/pallas_call | solution.py:259
  (99 shorter events, 29.2 us)
Async XLA Ops:
  3.5 40.5 %all-to-all-start = ((f32[16,200,128]{2,1,0:T(8,128)}), f32[16,200,128]{2,1,0:T(8,128)S(1)}, u32[]{:S(2)}, u32[]{:S(2)}) async-start(f32[16,200,128]{2,1,0:T(8,128)} %arrange_legendre.1), calls=%async_computation | async-start | bytes 3276800 | tf_op jit(solution)/shard_map/all_to_all | solution.py:281
  53.1 17.2 %collective-permute-start = (f32[8,320,128]{2,1,0:T(8,128)}, f32[8,320,128]{2,1,0:T(8,128)}, u32[]{:S(2)}, u32[]{:S(2)}) collective-permute-start(f32[8,320,128]{2,1,0:T(8,128)} %get-tuple-element.14), channel_id=1, source_target_pairs={{0,1},{1,0},{2,3},{3,2},{4,5},{5,4},{6,7},{7,6},{8,9},{9,8},{10,11... | collective-permute-start | bytes 3932168 | tf_op jit(solution)/shard_map/ppermute | solution.py:288
  53.9 9.7 %slice-start = ((s8[10485760]{0:T(1024)(128)(4,1)}), s8[4194304]{0:T(1024)(128)(4,1)S(1)}, s32[]{:S(2)}) async-start(s8[10485760]{0:T(1024)(128)(4,1)} %bitcast.69), calls=%async_computation.1 | async-start | bytes 8388608
  58.9 15.6 %collective-permute-start.5 = (f32[8,320,128]{2,1,0:T(8,128)}, f32[8,320,128]{2,1,0:T(8,128)}, u32[]{:S(2)}, u32[]{:S(2)}) collective-permute-start(f32[8,320,128]{2,1,0:T(8,128)} %get-tuple-element.16), channel_id=1, source_target_pairs={{0,1},{1,0},{2,3},{3,2},{4,5},{5,4},{6,7},{7,6},{8,9},{9,8},{10,11... | collective-permute-start | bytes 3932168 | tf_op jit(solution)/shard_map/ppermute | solution.py:288
  63.0 12.9 %collective-permute-start.10 = (f32[8,320,128]{2,1,0:T(8,128)}, f32[8,320,128]{2,1,0:T(8,128)}, u32[]{:S(2)}, u32[]{:S(2)}) collective-permute-start(f32[8,320,128]{2,1,0:T(8,128)} %get-tuple-element.18), channel_id=1, source_target_pairs={{0,1},{1,0},{2,3},{3,2},{4,5},{5,4},{6,7},{7,6},{8,9},{9,8},{10,11... | collective-permute-start | bytes 3932168 | tf_op jit(solution)/shard_map/ppermute | solution.py:288
  67.5 11.5 %collective-permute-start.15 = (f32[8,320,128]{2,1,0:T(8,128)}, f32[8,320,128]{2,1,0:T(8,128)}, u32[]{:S(2)}, u32[]{:S(2)}) collective-permute-start(f32[8,320,128]{2,1,0:T(8,128)} %get-tuple-element.20), channel_id=1, source_target_pairs={{0,1},{1,0},{2,3},{3,2},{4,5},{5,4},{6,7},{7,6},{8,9},{9,8},{10,11... | collective-permute-start | bytes 3932168 | tf_op jit(solution)/shard_map/ppermute | solution.py:288
  71.7 18.4 %collective-permute-start.1 = (f32[4,320,128]{2,1,0:T(8,128)S(1)}, f32[4,320,128]{2,1,0:T(8,128)S(1)}, u32[]{:S(2)}, u32[]{:S(2)}) collective-permute-start(f32[4,320,128]{2,1,0:T(8,128)S(1)} %slice_add_fusion.6), channel_id=1, source_target_pairs={{0,2},{1,3},{2,0},{3,1},{4,6},{5,7},{6,4},{7,5},{8,10},{9,11},{10,... | collective-permute-start | bytes 1966088 | tf_op jit(solution)/shard_map/ppermute | solution.py:288
  75.7 28.5 %collective-permute-start.6 = (f32[4,320,128]{2,1,0:T(8,128)S(1)}, f32[4,320,128]{2,1,0:T(8,128)S(1)}, u32[]{:S(2)}, u32[]{:S(2)}) collective-permute-start(f32[4,320,128]{2,1,0:T(8,128)S(1)} %slice_add_fusion.4), channel_id=1, source_target_pairs={{0,2},{1,3},{2,0},{3,1},{4,6},{5,7},{6,4},{7,5},{8,10},{9,11},{10,... | collective-permute-start | bytes 1966088 | tf_op jit(solution)/shard_map/ppermute | solution.py:288
  77.0 13.1 %copy-start.7 = (f32[8,320,128]{2,1,0:T(8,128)S(1)}, f32[8,320,128]{2,1,0:T(8,128)}, u32[]{:S(2)}) copy-start(f32[8,320,128]{2,1,0:T(8,128)} %copy-done.6) | copy-start | bytes 3932164
  77.0 41.2 %collective-permute-start.11 = (f32[4,320,128]{2,1,0:T(8,128)S(1)}, f32[4,320,128]{2,1,0:T(8,128)S(1)}, u32[]{:S(2)}, u32[]{:S(2)}) collective-permute-start(f32[4,320,128]{2,1,0:T(8,128)S(1)} %slice_add_fusion.2), channel_id=1, source_target_pairs={{0,2},{1,3},{2,0},{3,1},{4,6},{5,7},{6,4},{7,5},{8,10},{9,11},{10,... | collective-permute-start | bytes 1966088 | tf_op jit(solution)/shard_map/ppermute | solution.py:288
  80.2 51.9 %collective-permute-start.16 = (f32[4,320,128]{2,1,0:T(8,128)S(1)}, f32[4,320,128]{2,1,0:T(8,128)S(1)}, u32[]{:S(2)}, u32[]{:S(2)}) collective-permute-start(f32[4,320,128]{2,1,0:T(8,128)S(1)} %slice_add_fusion), channel_id=1, source_target_pairs={{0,2},{1,3},{2,0},{3,1},{4,6},{5,7},{6,4},{7,5},{8,10},{9,11},{10,... | collective-permute-start | bytes 1966088 | tf_op jit(solution)/shard_map/ppermute | solution.py:288
  91.4 47.7 %collective-permute-start.2 = (f32[320,128]{1,0:T(8,128)S(1)}, f32[320,128]{1,0:T(8,128)S(1)}, u32[]{:S(2)}, u32[]{:S(2)}) collective-permute-start(f32[320,128]{1,0:T(8,128)S(1)} %get-tuple-element.21), channel_id=1, source_target_pairs={{0,4},{1,5},{2,6},{3,7},{4,0},{5,1},{6,2},{7,3},{8,12},{9,13},{10,... | collective-permute-start | bytes 491528 | tf_op jit(solution)/shard_map/ppermute | solution.py:288
  96.1 44.2 %collective-permute-start.3 = (f32[320,128]{1,0:T(8,128)S(1)}, f32[320,128]{1,0:T(8,128)S(1)}, u32[]{:S(2)}, u32[]{:S(2)}) collective-permute-start(f32[320,128]{1,0:T(8,128)S(1)} %get-tuple-element.23), channel_id=1, source_target_pairs={{0,8},{1,9},{2,10},{3,11},{4,12},{5,13},{6,14},{7,15},{8,0},{9,1},... | collective-permute-start | bytes 491528 | tf_op jit(solution)/shard_map/ppermute | solution.py:288
  104.1 36.1 %collective-permute-start.4 = (f32[320,128]{1,0:T(8,128)S(1)}, f32[320,128]{1,0:T(8,128)S(1)}, u32[]{:S(2)}, u32[]{:S(2)}) collective-permute-start(f32[320,128]{1,0:T(8,128)S(1)} %get-tuple-element.22), channel_id=1, source_target_pairs={{0,12},{1,13},{2,14},{3,15},{4,8},{5,9},{6,10},{7,11},{8,4},{9,5},... | collective-permute-start | bytes 491528 | tf_op jit(solution)/shard_map/ppermute | solution.py:288
  118.2 25.4 %collective-permute-start.7 = (f32[320,128]{1,0:T(8,128)S(1)}, f32[320,128]{1,0:T(8,128)S(1)}, u32[]{:S(2)}, u32[]{:S(2)}) collective-permute-start(f32[320,128]{1,0:T(8,128)S(1)} %get-tuple-element.24), channel_id=1, source_target_pairs={{0,4},{1,5},{2,6},{3,7},{4,0},{5,1},{6,2},{7,3},{8,12},{9,13},{10,... | collective-permute-start | bytes 491528 | tf_op jit(solution)/shard_map/ppermute | solution.py:288
  132.0 23.3 %collective-permute-start.8 = (f32[320,128]{1,0:T(8,128)S(1)}, f32[320,128]{1,0:T(8,128)S(1)}, u32[]{:S(2)}, u32[]{:S(2)}) collective-permute-start(f32[320,128]{1,0:T(8,128)S(1)} %get-tuple-element.26), channel_id=1, source_target_pairs={{0,8},{1,9},{2,10},{3,11},{4,12},{5,13},{6,14},{7,15},{8,0},{9,1},... | collective-permute-start | bytes 491528 | tf_op jit(solution)/shard_map/ppermute | solution.py:288
  139.1 16.3 %collective-permute-start.9 = (f32[320,128]{1,0:T(8,128)S(1)}, f32[320,128]{1,0:T(8,128)S(1)}, u32[]{:S(2)}, u32[]{:S(2)}) collective-permute-start(f32[320,128]{1,0:T(8,128)S(1)} %get-tuple-element.25), channel_id=1, source_target_pairs={{0,12},{1,13},{2,14},{3,15},{4,8},{5,9},{6,10},{7,11},{8,4},{9,5},... | collective-permute-start | bytes 491528 | tf_op jit(solution)/shard_map/ppermute | solution.py:288
  140.2 21.5 %collective-permute-start.12 = (f32[320,128]{1,0:T(8,128)S(1)}, f32[320,128]{1,0:T(8,128)S(1)}, u32[]{:S(2)}, u32[]{:S(2)}) collective-permute-start(f32[320,128]{1,0:T(8,128)S(1)} %get-tuple-element.27), channel_id=1, source_target_pairs={{0,4},{1,5},{2,6},{3,7},{4,0},{5,1},{6,2},{7,3},{8,12},{9,13},{10,... | collective-permute-start | bytes 491528 | tf_op jit(solution)/shard_map/ppermute | solution.py:288
  140.3 30.8 %collective-permute-start.13 = (f32[320,128]{1,0:T(8,128)S(1)}, f32[320,128]{1,0:T(8,128)S(1)}, u32[]{:S(2)}, u32[]{:S(2)}) collective-permute-start(f32[320,128]{1,0:T(8,128)S(1)} %get-tuple-element.29), channel_id=1, source_target_pairs={{0,8},{1,9},{2,10},{3,11},{4,12},{5,13},{6,14},{7,15},{8,0},{9,1},... | collective-permute-start | bytes 491528 | tf_op jit(solution)/shard_map/ppermute | solution.py:288
  143.6 27.4 %collective-permute-start.14 = (f32[320,128]{1,0:T(8,128)S(1)}, f32[320,128]{1,0:T(8,128)S(1)}, u32[]{:S(2)}, u32[]{:S(2)}) collective-permute-start(f32[320,128]{1,0:T(8,128)S(1)} %get-tuple-element.28), channel_id=1, source_target_pairs={{0,12},{1,13},{2,14},{3,15},{4,8},{5,9},{6,10},{7,11},{8,4},{9,5},... | collective-permute-start | bytes 491528 | tf_op jit(solution)/shard_map/ppermute | solution.py:288
  155.4 15.7 %collective-permute-start.17 = (f32[320,128]{1,0:T(8,128)S(1)}, f32[320,128]{1,0:T(8,128)S(1)}, u32[]{:S(2)}, u32[]{:S(2)}) collective-permute-start(f32[320,128]{1,0:T(8,128)S(1)} %get-tuple-element.30), channel_id=1, source_target_pairs={{0,4},{1,5},{2,6},{3,7},{4,0},{5,1},{6,2},{7,3},{8,12},{9,13},{10,... | collective-permute-start | bytes 491528 | tf_op jit(solution)/shard_map/ppermute | solution.py:288
  155.4 22.7 %collective-permute-start.18 = (f32[320,128]{1,0:T(8,128)S(1)}, f32[320,128]{1,0:T(8,128)S(1)}, u32[]{:S(2)}, u32[]{:S(2)}) collective-permute-start(f32[320,128]{1,0:T(8,128)S(1)} %get-tuple-element.32), channel_id=1, source_target_pairs={{0,8},{1,9},{2,10},{3,11},{4,12},{5,13},{6,14},{7,15},{8,0},{9,1},... | collective-permute-start | bytes 491528 | tf_op jit(solution)/shard_map/ppermute | solution.py:288
  161.7 16.5 %copy-start.8 = (f32[128]{0:T(128)S(1)}, f32[128]{0:T(128)}, u32[]{:S(2)}) copy-start(f32[128]{0:T(128)} %param.11) | copy-start | bytes 1540
  161.7 16.3 %collective-permute-start.19 = (f32[320,128]{1,0:T(8,128)S(1)}, f32[320,128]{1,0:T(8,128)S(1)}, u32[]{:S(2)}, u32[]{:S(2)}) collective-permute-start(f32[320,128]{1,0:T(8,128)S(1)} %get-tuple-element.31), channel_id=1, source_target_pairs={{0,12},{1,13},{2,14},{3,15},{4,8},{5,9},{6,10},{7,11},{8,4},{9,5},... | collective-permute-start | bytes 491528 | tf_op jit(solution)/shard_map/ppermute | solution.py:288
  (12 other events, 57.8 us)

commit v2 on v1

v2 whole, which is shorter than its diff:
```python
import functools
import math

import jax
import jax.numpy as jnp
from jax import lax
from jax.experimental import pallas as pl
from jax.experimental.pallas import tpu as pltpu
from jax.sharding import PartitionSpec as P

NLON = 1280
STEP = 32
PLANES = 4
LANES = 128

PRECISE = lax.Precision.HIGHEST
F32 = jnp.float32
BF16 = jnp.bfloat16


def prior_scale(shard, first):
    waves = shard.shape[0]
    slots = shard.shape[2]
    orders = jnp.arange(waves, dtype=jnp.int32)[:, None, None]
    parity = jnp.arange(2, dtype=jnp.int32)[None, :, None]
    slot_index = first + jnp.arange(slots, dtype=jnp.int32)[None, None, :]
    degree = orders + 2 * slot_index + parity
    spread = lax.rsqrt((degree + 1).astype(F32) * waves)
    spread = jnp.where(degree < waves, spread, jnp.zeros_like(spread))
    return shard.astype(F32) * spread[..., None]


def channel_kernel(peak_level, width, levels):
    height = jnp.arange(levels, dtype=F32)[:, None]
    offsets = (height - peak_level.astype(F32)[None, :]) / width[None, :]
    weights = jnp.exp(-offsets * offsets)
    return weights / jnp.sum(weights, axis=0, keepdims=True)


def radiate(temps, absorb, kernel):
    levels = temps.shape[-1]
    strict_upper = (jnp.arange(levels)[:, None] < jnp.arange(levels)[None, :]).astype(F32)
    source = jnp.exp(0.5 * temps)
    layers = absorb[None, :] * source
    overhead = jnp.dot(layers, strict_upper, precision=PRECISE, preferred_element_type=F32)
    emitted = source * jnp.exp(-overhead) * -jnp.expm1(-layers)
    return jnp.dot(emitted, kernel, precision=PRECISE, preferred_element_type=F32)


def fourier_lookup(row_count, waves, points):
    orders = jnp.arange(waves, dtype=jnp.int32)
    places = jnp.arange(points, dtype=jnp.int32)
    phases = places[:, None] * orders[None, :] % row_count
    angles = 2.0 * math.pi * phases.astype(F32) / row_count.astype(F32)
    weights = jnp.where(orders == 0, 1.0, 2.0) * (2 * orders < row_count).astype(F32)
    return jnp.stack((weights * jnp.cos(angles), -weights * jnp.sin(angles)), axis=-1)


def synthesize_row(spectra, row_count, modes_basis, absorb, kernel, points):
    waves, hemis, columns = spectra.shape
    lookup = fourier_lookup(row_count, waves, points)
    split_parts = spectra.reshape(waves, hemis, 2, columns // 2)
    fields = jnp.einsum("kmq,mhqc->hkc", lookup, split_parts, precision=PRECISE)
    fields = jnp.einsum("hkc,cl->hkl", fields, modes_basis, precision=PRECISE)
    levels = fields.shape[-1]
    bright = radiate(fields.reshape(hemis * points, levels), absorb, kernel)
    bright = bright.reshape(hemis, points, kernel.shape[1])
    inside = (jnp.arange(points, dtype=jnp.int32) < row_count).astype(F32)
    return bright * inside[None, :, None]


def legendre_rows(legendre, spectral):
    even_odd = jnp.einsum("mpsj,mpsc->mpjc", legendre, spectral, precision=PRECISE)
    return jnp.stack((even_odd[:, 0] + even_odd[:, 1], even_odd[:, 0] - even_odd[:, 1]), axis=1)


def move_coefficients(coefficients, legendre, row_counts, basis, absorb, peak_level, width):
    first = lax.axis_index("spec") * coefficients.shape[2]
    scaled = prior_scale(coefficients, first)
    kernel = channel_kernel(peak_level, width, basis.shape[1])
    spectral = lax.all_to_all(scaled, "spec", split_axis=0, concat_axis=2, tiled=True)
    fourier = legendre_rows(legendre, spectral)
    pieces = lax.all_to_all(fourier, "spec", split_axis=2, concat_axis=0, tiled=True)
    row = synthesize_row(pieces[:, :, 0, :], row_counts[0], basis, absorb, kernel, NLON)
    return row[None]


def split_pair(value):
    high = value.astype(BF16)
    return high, (value - high.astype(F32)).astype(BF16)


def split_constant(value):
    high = lax.reduce_precision(value, exponent_bits=8, mantissa_bits=7)
    return high.astype(BF16), (value - high).astype(BF16)


def arrange_legendre(legendre, me, spec, waves):
    held, _, slots, rows = legendre.shape
    groups, own = held // 4, slots // spec
    lanes = rows * 8

    def body(me_ref, leg_ref, out_ref, turned):
        pair = lax.broadcasted_iota(jnp.int32, (8, slots), 0)
        slot = lax.broadcasted_iota(jnp.int32, (8, slots), 1)
        for group in range(groups):
            degree = me_ref[0] * held + 4 * group + pair // 2 + 2 * slot + pair % 2
            spread = lax.rsqrt((degree + 1).astype(F32) * waves)
            spread = jnp.where(degree < waves, spread, 0.0)
            block = leg_ref[4 * group:4 * group + 4].reshape(8, rows, slots)
            block = block * spread[:, None, :]
            block = jnp.swapaxes(block, 0, 1).reshape(lanes, slots)
            turned[...] = block.T
            for goal in range(spec):
                piece = turned[goal * own:(goal + 1) * own, :]
                out_ref[goal, group * own:(group + 1) * own, :] = piece

    return pl.pallas_call(
        body,
        grid_spec=pltpu.PrefetchScalarGridSpec(
            num_scalar_prefetch=1,
            grid=(1,),
            in_specs=[pl.BlockSpec((held, 2, rows, slots), lambda i, f: (0, 0, 0, 0))],
            out_specs=pl.BlockSpec((spec, groups * own, lanes), lambda i, f: (0, 0, 0)),
            scratch_shapes=[pltpu.VMEM((slots, lanes), F32)],
        ),
        out_shape=jax.ShapeDtypeStruct((spec, groups * own, lanes), F32),
        compiler_params=pltpu.CompilerParams(vmem_limit_bytes=32 << 20),
        cost_estimate=pl.CostEstimate(flops=1, bytes_accessed=1, transcendentals=0),
        name="arrange_legendre",
    )(me[None], jnp.transpose(legendre, (0, 1, 3, 2)))


def partial_rows(order, arranged, coefficients, plane, own):
    spec, depth, lanes = arranged.shape
    sources = spec // PLANES
    groups = depth // own
    half = lanes // 16
    columns = coefficients.shape[-1]
    span = 8 * own

    def body(order_ref, leg_ref, coef_ref, keep_ref, send_ref, spread_ref):
        row = lax.broadcasted_iota(jnp.int32, (lanes, span), 0) % 8
        inner = lax.broadcasted_iota(jnp.int32, (lanes, span), 1)
        here = row == 2 * (inner // (2 * own)) + inner % 2
        first_core = jnp.full((8, columns), order_ref[half], jnp.int32) == 0
        for group in range(groups):
            piece = leg_ref[0, group * own:(group + 1) * own, :]
            for copy in range(4):
                for parity in range(2):
                    spread_ref[pl.ds(2 * own * copy + parity, own, stride=2), :] = piece
            high, low = split_pair(jnp.where(here, spread_ref[...].T, 0.0))
            coef = coef_ref[span * group:span * (group + 1), :]
            total = jnp.dot(high, coef, preferred_element_type=F32) + jnp.dot(low, coef, preferred_element_type=F32)
            for couple in range(half):
                one = total[16 * couple:16 * couple + 8]
                two = total[16 * couple + 8:16 * couple + 16]
                place = order_ref[couple]
                keep_ref[place, 8 * group:8 * group + 8, :] = jnp.where(first_core, one, two)
                send_ref[place, 8 * group:8 * group + 8, :] = jnp.where(first_core, two, one)

    out = jax.ShapeDtypeStruct((half, sources * groups * 8, columns), F32)
    out_spec = pl.BlockSpec((half, groups * 8, columns), lambda i, o: (0, i, 0))
    return pl.pallas_call(
        body,
        grid_spec=pltpu.PrefetchScalarGridSpec(
            num_scalar_prefetch=1,
            grid=(sources,),
            in_specs=[
                pl.BlockSpec((1, depth, lanes), lambda i, o: (plane * sources + i, 0, 0)),
                pl.BlockSpec((groups * span, columns), lambda i, o: (plane * sources + i, 0)),
            ],
            out_specs=[out_spec, out_spec],
            scratch_shapes=[pltpu.VMEM((span, lanes), F32)],
        ),
        out_shape=[out, out],
        compiler_params=pltpu.CompilerParams(vmem_limit_bytes=32 << 20),
        cost_estimate=pl.CostEstimate(flops=1, bytes_accessed=1, transcendentals=0),
        name="partial_rows",
    )(order, arranged, coefficients)


def wave_tables(row_count, waves):
    orders = jnp.arange(waves, dtype=jnp.int32)
    weights = jnp.where(orders == 0, 1.0, 2.0) * (2 * orders < row_count).astype(F32)
    steps = NLON // STEP
    coarse = STEP * jnp.arange(steps, dtype=jnp.int32)
    places = jnp.concatenate((coarse, jnp.arange(STEP, dtype=jnp.int32)))
    phases = places[:, None] * orders[None, :] % row_count
    angles = 2.0 * math.pi * phases.astype(F32) / row_count.astype(F32)
    gain = jnp.where(jnp.arange(places.shape[0])[:, None] < steps, weights[None, :], 1.0)
    bases = (gain * jnp.cos(angles), gain * jnp.sin(angles))
    parts = 8

    def body(cos_ref, sin_ref, ch_ref, cl_ref, sh_ref, sl_ref):
        cos_fine, sin_fine = cos_ref[steps:, :], sin_ref[steps:, :]
        for part in range(parts):
            at = pl.program_id(0) * parts + part
            cos_at, sin_at = cos_ref[pl.ds(at, 1), :], sin_ref[pl.ds(at, 1), :]
            here = slice(part * STEP, (part + 1) * STEP)
            ch_ref[here, :], cl_ref[here, :] = split_pair(cos_at * cos_fine - sin_at * sin_fine)
            sh_ref[here, :], sl_ref[here, :] = split_pair(sin_at * cos_fine + cos_at * sin_fine)

    tile = parts * STEP
    return pl.pallas_call(
        body,
        grid=(NLON // tile,),
        in_specs=[pl.BlockSpec(bases[0].shape, lambda i: (0, 0))] * 2,
        out_specs=[pl.BlockSpec((tile, waves), lambda i: (i, 0))] * 4,
        out_shape=[jax.ShapeDtypeStruct((NLON, waves), BF16)] * 4,
        compiler_params=pltpu.CompilerParams(vmem_limit_bytes=32 << 20),
        cost_estimate=pl.CostEstimate(flops=1, bytes_accessed=1, transcendentals=0),
        name="wave_tables",
    )(*bases)


def synthesize(scalars, spectra, tables, basis, absorb, kernel):
    planes, deep, columns = spectra.shape
    span = deep // 2
    waves = planes * span
    levels = basis.shape[1]
    channels = kernel.shape[1]
    tile = 8 * STEP
    zero = jnp.zeros_like(basis)
    widened = jnp.concatenate((basis, zero, zero, -basis), axis=0)
    basis_high, basis_low = split_constant(widened)
    kernel_high, kernel_low = split_constant(kernel)

    def body(scalar_ref, spec_ref, ch_ref, cl_ref, sh_ref, sl_ref, bh_ref, bl_ref, ab_ref, kh_ref, kl_ref,
             out_ref, high_ref, low_ref):
        step = pl.program_id(0)

        @pl.when(step == 0)
        def _():
            for plane in range(planes):
                here = pl.ds(pl.multiple_of(scalar_ref[1 + plane] * span, 16), span)
                for parity in range(2):
                    high, low = split_pair(spec_ref[plane, pl.ds(parity, span, stride=2), :])
                    high_ref[here, parity * columns:(parity + 1) * columns] = high
                    low_ref[here, parity * columns:(parity + 1) * columns] = low

        sides = []
        for first_ref, second_ref in ((ch_ref, cl_ref), (sh_ref, sl_ref)):
            fields = jnp.dot(first_ref[...], high_ref[...], preferred_element_type=F32)
            fields += jnp.dot(second_ref[...], high_ref[...], preferred_element_type=F32)
            fields += jnp.dot(first_ref[...], low_ref[...], preferred_element_type=F32)
            even, odd = fields[:, :columns], fields[:, columns:]
            sides.append((even + odd, even - odd))
        both = jnp.concatenate(
            [jnp.concatenate([sides[0][side], sides[1][side]], axis=1) for side in range(2)], axis=0
        )
        high, low = split_pair(both)
        temps = jnp.dot(high, bh_ref[...], preferred_element_type=F32)
        temps += jnp.dot(low, bh_ref[...], preferred_element_type=F32)
        temps += jnp.dot(high, bl_ref[...], preferred_element_type=F32)
        source = jnp.exp(0.5 * temps)
        layers = ab_ref[...] * source
        above = lax.broadcasted_iota(jnp.int32, (2 * levels, levels), 0) % levels
        level = lax.broadcasted_iota(jnp.int32, (2 * levels, levels), 1)
        upper = jnp.where(above < level, 1.0, 0.0).astype(BF16)
        overhead = jnp.dot(jnp.concatenate(split_pair(layers), axis=1), upper, preferred_element_type=F32)
        half = jnp.tanh(0.5 * layers)
        emitted = source * jnp.exp(-overhead) * (2.0 * half / (1.0 + half))
        high, low = split_pair(emitted)
        bright = jnp.dot(high, kh_ref[...], preferred_element_type=F32)
        bright += jnp.dot(low, kh_ref[...], preferred_element_type=F32)
        bright += jnp.dot(high, kl_ref[...], preferred_element_type=F32)
        place = step * tile + lax.broadcasted_iota(jnp.int32, (2 * tile, 1), 0) % tile
        bright = jnp.where(place < scalar_ref[0], bright, 0.0)
        out_ref[0] = bright.reshape(2, tile, channels)

    def whole(array):
        return pl.BlockSpec(array.shape, lambda i, c: (0,) * array.ndim)

    constants = (basis_high, basis_low, absorb[None, :], kernel_high, kernel_low)
    table_spec = pl.BlockSpec((tile, waves), lambda i, c: (i, 0))
    return pl.pallas_call(
        body,
        grid_spec=pltpu.PrefetchScalarGridSpec(
            num_scalar_prefetch=1,
            grid=(NLON // tile,),
            in_specs=[whole(spectra)] + [table_spec] * 4 + [whole(array) for array in constants],
            out_specs=pl.BlockSpec((1, 2, tile, channels), lambda i, c: (0, 0, i, 0)),
            scratch_shapes=[pltpu.VMEM((waves, 2 * columns), BF16)] * 2,
        ),
        out_shape=jax.ShapeDtypeStruct((1, 2, NLON, channels), F32),
        compiler_params=pltpu.CompilerParams(vmem_limit_bytes=48 << 20),
        cost_estimate=pl.CostEstimate(flops=1, bytes_accessed=1, transcendentals=0),
        name="synthesize",
    )(scalars, spectra, *tables, *constants)


def move_legendre(spec, coefficients, legendre, row_counts, basis, absorb, peak_level, width):
    waves, _, own, columns = coefficients.shape
    held = legendre.shape[0]
    sources = spec // PLANES
    quarter = spec // 4
    me = lax.axis_index("spec").astype(jnp.int32)
    natural = jnp.transpose(coefficients, (0, 2, 1, 3)).reshape(waves * 2 * own, columns)

    def swap(value, distance, use=None):
        pairs = [(i, i ^ distance) for i in range(spec) if use is None or use(i)]
        return lax.ppermute(value, "spec", pairs)

    def after(values, earlier):
        return lax.optimization_barrier((values, earlier))[0]

    arranged = arrange_legendre(legendre, me, spec, waves)
    tables = wave_tables(row_counts[0], waves)
    kernel = channel_kernel(peak_level, width, basis.shape[1])
    arrived = lax.all_to_all(arranged, "spec", split_axis=0, concat_axis=0, tiled=True)
    arrived = after(arrived, (tables, kernel))
    couple = jnp.arange(spec // 2, dtype=jnp.int32) ^ (me >> 1)
    order = jnp.concatenate(((couple & 1) * quarter + (couple >> 1), (me & 1)[None]))

    def contract(plane, earlier=()):
        return partial_rows(after(order, earlier), arrived, natural, plane, own)

    def add_cores(keep, other):
        return keep[quarter:] + other[quarter:], keep[:quarter] + other[:quarter]

    def between_planes(value, plane):
        use = lambda i: (plane * held + 2 * (i // sources) * own) * sources < waves
        return [swap(value[away], sources * away, use) for away in range(1, PLANES)]

    keep3, send3 = contract(3)
    keep0, send0 = contract(0, send3)
    keep1, send1 = contract(1, send0)
    both3 = keep3 + swap(send3, 1)
    early = between_planes(jnp.swapaxes(both3.reshape(2, quarter, *both3.shape[1:]), 0, 1), 3)
    side0, own0 = add_cores(keep0, swap(send0, 1))
    keep2, send2 = contract(2, (side0, both3, send1))
    sum0 = own0 + swap(side0, 2)
    side1, own1 = add_cores(keep1, swap(send1, 1))
    late0 = between_planes(sum0, 0)

    keep2, other2 = after((keep2, swap(send2, 1)), (sum0, side1))
    side2, own2 = add_cores(keep2, other2)
    sum1 = own1 + swap(side1, 2)
    late1 = between_planes(sum1, 1)
    sum3 = both3.reshape(2, quarter, *both3.shape[1:])[:, 0] + sum(early)
    sum3 = sum3[0] + swap(after(sum3[1], side2), 2)
    sum2 = own2 + swap(side2, 2)
    late2 = between_planes(after(sum2, late0), 2)
    spectra = jnp.stack([sum0[0] + sum(late0), sum1[0] + sum(late1), sum2[0] + sum(late2), sum3])
    scalars = jnp.concatenate((row_counts, jnp.arange(PLANES, dtype=jnp.int32)))
    return synthesize(scalars, spectra, tables, basis, absorb, kernel)


def solution(mesh):
    spec = mesh.shape["spec"]
    placed = (
        P("draws", None, "spec", None),
        P("spec", None, None, None),
        P("spec"),
        P(),
        P(),
        P(),
        P(),
    )

    def on_device(coefficients, legendre, *others):
        held, _, _, rows = legendre.shape
        own = coefficients.shape[2]
        if rows == spec and 8 * rows == LANES and held % 8 == 0 and rows <= own:
            return move_legendre(spec, coefficients, legendre, *others)
        return move_coefficients(coefficients, legendre, *others)

    return jax.shard_map(
        on_device,
        mesh=mesh,
        in_specs=placed,
        out_specs=P(("draws", "spec"), None, None, None),
        check_vma=False,
    )
```

time: 197 us -> 151 us (0.77)
  the two profiles are of different devices: /device:TPU:0 before, /device:TPU:23 now
where the time goes in v2:
time: 151 us
  waiting for transfers between devices  68.3 us (45%)
  starting transfers between devices  39 us (26%)
  Pallas kernels  30.3 us (20%)
  local copies, waits for them, and re-layouts  8.33 us (6%)
  other arithmetic  4.08 us (3%)
    ppermute x20, waiting for transfers between devices, swap(): return lax.ppermute(value, 'spec', pairs)  41.4 us
    ppermute x20, starting transfers between devices, swap(): return lax.ppermute(value, 'spec', pairs)  32.6 us
    all_to_all x1, waiting for transfers between devices, move_legendre(): lax.all_to_all(arranged, 'spec', split_axis=0, concat_axis=0, tiled=True)  26.9 us
    pallas_call x4, Pallas kernels, partial_rows(): pl.pallas_call(body, grid_spec=pltpu.PrefetchScalarGridSpec(num_scalar_pr...  13.6 us
    pallas_call x1, Pallas kernels, synthesize(): pl.pallas_call(body, grid_spec=pltpu.PrefetchScalarGridSpec(num_scalar_pr...  13 us
    unnamed x22, local copies, waits for them, and re-layouts  7.98 us
    all_to_all x1, starting transfers between devices, move_legendre(): lax.all_to_all(arranged, 'spec', split_axis=0, concat_axis=0, tiled=True)  6.44 us
  transfers between devices with their start and end apart: 21, of which 8 were waited for; matrix products, arithmetic and copies ran while one was open for 3% of the time, Pallas kernels for 8%

profile of v2, /device:TPU:23, one launch (start us, length us, event | category | flops | bytes accessed | tf_op | source)
XLA Modules:
  0.0 151.0 jit_solution(13490920121391339631)
XLA Ops:
  0.0 1.5 %copy-done.1 = f32[40,2,320,16]{2,3,1,0:T(8,128)S(1)} copy-done((f32[40,2,320,16]{2,3,1,0:T(8,128)S(1)}, f32[40,2,320,16]{2,3,1,0:T(8,128)}, u32[]{:S(2)}) %copy-start.1) | copy-done | bytes 1638424
  1.5 2.0 %arrange_legendre.1 = f32[16,200,128]{2,1,0:T(8,128)} custom-call(s32[1]{0:T(128)} %bitcast.1.me_ref, f32[40,2,16,320]{3,2,1,0:T(8,128)S(1)} %bitcast.82), custom_call_target="tpu_custom_call" | custom-call | flops 1 | bytes 1 | tf_op jit(solution)/shard_map/arrange_legendre/pallas_call | solution.py:118
  3.5 6.4 %all-to-all-start = ((f32[16,200,128]{2,1,0:T(8,128)}), f32[16,200,128]{2,1,0:T(8,128)S(1)}, u32[]{:S(2)}, u32[]{:S(2)}) async-start(f32[16,200,128]{2,1,0:T(8,128)} %arrange_legendre.1), calls=%async_computation | async-start | bytes 3276800 | tf_op jit(solution)/shard_map/all_to_all | solution.py:311
  10.7 2.6 %select_multiply_fusion = (f32[72,640]{1,0:T(8,128)S(1)}, f32[72,640]{1,0:T(8,128)S(1)}) fusion(f32[640]{0:T(1024)S(1)} %select_select_fusion, pred[72]{0:T(512)(128)(4,1)S(1)} %iota_compare_fusion.1, f32[]{:T(128)S(6)} %convert_element_type.23, pred[]{:T(512)S(6)} %lt.34, s32[]{:T(128)S(6)} %select_n.23, s32[72]{0:T(128)S(1)} %pad_add_fusion.2), kind=kLoop, calls=%fused_computation.18 | loop fusion | flops 645120 | bytes 371569 | tf_op jit(solution)/shard_map/mul | solution.py:192
  13.3 1.7 %wave_tables.1 = (bf16[1280,640]{1,0:T(8,128)(2,1)S(1)}, bf16[1280,640]{1,0:T(8,128)(2,1)S(1)}, bf16[1280,640]{1,0:T(8,128)(2,1)S(1)}, bf16[1280,640]{1,0:T(8,128)(2,1)S(1)}) custom-call(f32[72,640]{1,0:T(8,128)S(1)} %get-tuple-element.64.cos_ref, f32[72,640]{1,0:T(8,128)S(1)} %get-tuple-element.63.sin_ref), custom_call_target="tpu_custom_call" | custom-call | flops 1 | bytes 1 | tf_op jit(solution)/shard_map/wave_tables/pallas_call | solution.py:205
  18.7 26.9 %all-to-all-done.leg_ref = f32[16,200,128]{2,1,0:T(8,128)S(1)} async-done(((f32[16,200,128]{2,1,0:T(8,128)}), f32[16,200,128]{2,1,0:T(8,128)S(1)}, u32[]{:S(2)}, u32[]{:S(2)}) %all-to-all-start) | async-done | bytes 1638432 | tf_op jit(solution)/shard_map/all_to_all | solution.py:311
  45.6 2.9 %copy-done = bf16[640,2,20,128]{3,1,2,0:T(2,128)(2,1)S(1)} copy-done((bf16[640,2,20,128]{3,1,2,0:T(2,128)(2,1)S(1)}, bf16[640,2,20,128]{3,1,2,0:T(2,128)(2,1)}, u32[]{:S(2)}) %copy-start) | copy-done | bytes 6553624
  48.4 3.4 %partial_rows.4 = (f32[8,320,128]{2,1,0:T(8,128)S(1)}, f32[8,320,128]{2,1,0:T(8,128)S(1)}) custom-call(s32[9]{0:T(128)S(1)} %pad_add_fusion.1.order_ref, f32[16,200,128]{2,1,0:T(8,128)S(1)} %all-to-all-done.leg_ref, bf16[25600,128]{1,0:T(8,128)(2,1)S(1)} %bitcast.78), custom_call_target="tpu_custom_call" | custom-call | flops 1 | bytes 1 | tf_op jit(solution)/shard_map/partial_rows/pallas_call | solution.py:164
  52.8 3.4 %partial_rows.5 = (f32[8,320,128]{2,1,0:T(8,128)S(1)}, f32[8,320,128]{2,1,0:T(8,128)S(1)}) custom-call(s32[9]{0:T(128)S(1)} %pad_add_fusion.1.order_ref, f32[16,200,128]{2,1,0:T(8,128)S(1)} %all-to-all-done.leg_ref, bf16[25600,128]{1,0:T(8,128)(2,1)S(1)} %bitcast.79), custom_call_target="tpu_custom_call" | custom-call | flops 1 | bytes 1 | tf_op jit(solution)/shard_map/partial_rows/pallas_call | solution.py:164
  56.3 3.4 %partial_rows.6 = (f32[8,320,128]{2,1,0:T(8,128)S(1)}, f32[8,320,128]{2,1,0:T(8,128)S(1)}) custom-call(s32[9]{0:T(128)S(1)} %pad_add_fusion.1.order_ref, f32[16,200,128]{2,1,0:T(8,128)S(1)} %all-to-all-done.leg_ref, bf16[25600,128]{1,0:T(8,128)(2,1)S(1)} %bitcast.80), custom_call_target="tpu_custom_call" | custom-call | flops 1 | bytes 1 | tf_op jit(solution)/shard_map/partial_rows/pallas_call | solution.py:164
  63.8 2.1 %collective-permute-start.1 = (f32[4,320,128]{2,1,0:T(8,128)S(1)}, f32[4,320,128]{2,1,0:T(8,128)S(1)}, u32[]{:S(2)}, u32[]{:S(2)}) collective-permute-start(f32[4,320,128]{2,1,0:T(8,128)S(1)} %slice_add_fusion.2), channel_id=1, source_target_pairs={{0,2},{1,3},{2,0},{3,1},{4,6},{5,7},{6,4},{7,5},{8,10},{9,11},{10,... | collective-permute-start | bytes 1966088 | tf_op jit(solution)/shard_map/ppermute | solution.py:303
  65.9 3.4 %partial_rows.7 = (f32[8,320,128]{2,1,0:T(8,128)S(1)}, f32[8,320,128]{2,1,0:T(8,128)S(1)}) custom-call(s32[9]{0:T(128)S(1)} %pad_add_fusion.1.order_ref, f32[16,200,128]{2,1,0:T(8,128)S(1)} %all-to-all-done.leg_ref, bf16[25600,128]{1,0:T(8,128)(2,1)S(1)} %bitcast.81), custom_call_target="tpu_custom_call" | custom-call | flops 1 | bytes 1 | tf_op jit(solution)/shard_map/partial_rows/pallas_call | solution.py:164
  69.8 3.4 %collective-permute-done.17 = f32[2,320,128]{2,1,0:T(8,128)S(1)} collective-permute-done((f32[2,320,128]{2,1,0:T(8,128)S(1)}, f32[2,320,128]{2,1,0:T(8,128)S(1)}, u32[]{:S(2)}, u32[]{:S(2)}) %collective-permute-start.17) | collective-permute-done | bytes 327712 | tf_op jit(solution)/shard_map/ppermute | solution.py:303
  73.2 2.0 %collective-permute-start.6 = (f32[4,320,128]{2,1,0:T(8,128)S(1)}, f32[4,320,128]{2,1,0:T(8,128)S(1)}, u32[]{:S(2)}, u32[]{:S(2)}) collective-permute-start(f32[4,320,128]{2,1,0:T(8,128)S(1)} %slice_add_fusion), channel_id=1, source_target_pairs={{0,2},{1,3},{2,0},{3,1},{4,6},{5,7},{6,4},{7,5},{8,10},{9,11},{10,... | collective-permute-start | bytes 1966088 | tf_op jit(solution)/shard_map/ppermute | solution.py:303
  75.3 5.7 %collective-permute-done.1 = f32[4,320,128]{2,1,0:T(8,128)S(1)} collective-permute-done((f32[4,320,128]{2,1,0:T(8,128)S(1)}, f32[4,320,128]{2,1,0:T(8,128)S(1)}, u32[]{:S(2)}, u32[]{:S(2)}) %collective-permute-start.1) | collective-permute-done | bytes 655392 | tf_op jit(solution)/shard_map/ppermute | solution.py:303
  81.1 6.7 %collective-permute-start.4 = (f32[320,128]{1,0:T(8,128)S(1)}, f32[320,128]{1,0:T(8,128)S(1)}, u32[]{:S(2)}, u32[]{:S(2)}) collective-permute-start(f32[320,128]{1,0:T(8,128)S(1)} %get-tuple-element.56), channel_id=1, source_target_pairs={{0,12},{1,13},{2,14},{3,15},{4,8},{5,9},{6,10},{7,11},{8,4},{9,5},... | collective-permute-start | bytes 491528 | tf_op jit(solution)/shard_map/ppermute | solution.py:303
  89.1 5.9 %collective-permute-done.6 = f32[4,320,128]{2,1,0:T(8,128)S(1)} collective-permute-done((f32[4,320,128]{2,1,0:T(8,128)S(1)}, f32[4,320,128]{2,1,0:T(8,128)S(1)}, u32[]{:S(2)}, u32[]{:S(2)}) %collective-permute-start.6) | collective-permute-done | bytes 655392 | tf_op jit(solution)/shard_map/ppermute | solution.py:303
  96.6 5.8 %collective-permute-start.8 = (f32[320,128]{1,0:T(8,128)S(1)}, f32[320,128]{1,0:T(8,128)S(1)}, u32[]{:S(2)}, u32[]{:S(2)}) collective-permute-start(f32[320,128]{1,0:T(8,128)S(1)} %get-tuple-element.50), channel_id=1, source_target_pairs={{0,8},{1,9},{2,10},{3,11},{4,12},{5,13},{6,14},{7,15},{8,0},{9,1},... | collective-permute-start | bytes 491528 | tf_op jit(solution)/shard_map/ppermute | solution.py:303
  102.4 1.9 %collective-permute-start.9 = (f32[320,128]{1,0:T(8,128)S(1)}, f32[320,128]{1,0:T(8,128)S(1)}, u32[]{:S(2)}, u32[]{:S(2)}) collective-permute-start(f32[320,128]{1,0:T(8,128)S(1)} %get-tuple-element.51), channel_id=1, source_target_pairs={{0,12},{1,13},{2,14},{3,15},{4,8},{5,9},{6,10},{7,11},{8,4},{9,5},... | collective-permute-start | bytes 491528 | tf_op jit(solution)/shard_map/ppermute | solution.py:303
  105.7 10.3 %collective-permute-done.9 = f32[320,128]{1,0:T(8,128)S(1)} collective-permute-done((f32[320,128]{1,0:T(8,128)S(1)}, f32[320,128]{1,0:T(8,128)S(1)}, u32[]{:S(2)}, u32[]{:S(2)}) %collective-permute-start.9) | collective-permute-done | bytes 163872 | tf_op jit(solution)/shard_map/ppermute | solution.py:303
  116.1 2.0 %collective-permute-start.19 = (f32[320,128]{1,0:T(8,128)S(1)}, f32[320,128]{1,0:T(8,128)S(1)}, u32[]{:S(2)}, u32[]{:S(2)}) collective-permute-start(f32[320,128]{1,0:T(8,128)S(1)} %slice_bitcast_fusion.4), channel_id=1, source_target_pairs={{0,2},{1,3},{2,0},{3,1},{4,6},{5,7},{6,4},{7,5},{8,10},{9,11},{10,... | collective-permute-start | bytes 491528 | tf_op jit(solution)/shard_map/ppermute | solution.py:303
  122.3 3.9 %collective-permute-done.14 = f32[320,128]{1,0:T(8,128)S(1)} collective-permute-done((f32[320,128]{1,0:T(8,128)S(1)}, f32[320,128]{1,0:T(8,128)S(1)}, u32[]{:S(2)}, u32[]{:S(2)}) %collective-permute-start.14) | collective-permute-done | bytes 163872 | tf_op jit(solution)/shard_map/ppermute | solution.py:303
  126.2 11.7 %collective-permute-done.15 = f32[320,128]{1,0:T(8,128)S(1)} collective-permute-done((f32[320,128]{1,0:T(8,128)S(1)}, f32[320,128]{1,0:T(8,128)S(1)}, u32[]{:S(2)}, u32[]{:S(2)}) %collective-permute-start.15) | collective-permute-done | bytes 163872 | tf_op jit(solution)/shard_map/ppermute | solution.py:303
  138.0 13.0 %synthesize.1 = f32[1,2,1280,512]{3,2,1,0:T(8,128)} custom-call(s32[5]{0:T(128)S(1)} %pad_add_fusion.scalar_ref, f32[4,320,128]{2,1,0:T(8,128)S(1)} %pad_maximum_fusion.spec_ref, bf16[1280,640]{1,0:T(8,128)(2,1)S(1)} %get-tuple-element.25.ch_ref, bf16[1280,640]{1,0:T(8,128)(2,1)S(1)} %copy-done.3, bf16[1280,640]{1,0:T(8,128)(2,1)S(1)} %copy-done.5, ...), custom_call_target="tpu_custom_call" | custom-call | flops 1 | bytes 1 | tf_op jit(solution)/shard_map/synthesize/pallas_call | solution.py:277
  (83 shorter events, 17.9 us)
Async XLA Ops:
  3.5 42.0 %all-to-all-start = ((f32[16,200,128]{2,1,0:T(8,128)}), f32[16,200,128]{2,1,0:T(8,128)S(1)}, u32[]{:S(2)}, u32[]{:S(2)}) async-start(f32[16,200,128]{2,1,0:T(8,128)} %arrange_legendre.1), calls=%async_computation | async-start | bytes 3276800 | tf_op jit(solution)/shard_map/all_to_all | solution.py:311
  51.8 8.9 %collective-permute-start.10 = (f32[8,320,128]{2,1,0:T(8,128)S(1)}, f32[8,320,128]{2,1,0:T(8,128)S(1)}, u32[]{:S(2)}, u32[]{:S(2)}) collective-permute-start(f32[8,320,128]{2,1,0:T(8,128)S(1)} %get-tuple-element.30), channel_id=1, source_target_pairs={{0,1},{1,0},{2,3},{3,2},{4,5},{5,4},{6,7},{7,6},{8,9},{9,8},{10,11... | collective-permute-start | bytes 3932168 | tf_op jit(solution)/shard_map/ppermute | solution.py:303
  56.2 7.6 %collective-permute-start = (f32[8,320,128]{2,1,0:T(8,128)S(1)}, f32[8,320,128]{2,1,0:T(8,128)S(1)}, u32[]{:S(2)}, u32[]{:S(2)}) collective-permute-start(f32[8,320,128]{2,1,0:T(8,128)S(1)} %get-tuple-element.33), channel_id=1, source_target_pairs={{0,1},{1,0},{2,3},{3,2},{4,5},{5,4},{6,7},{7,6},{8,9},{9,8},{10,11... | collective-permute-start | bytes 3932168 | tf_op jit(solution)/shard_map/ppermute | solution.py:303
  59.7 9.6 %collective-permute-start.5 = (f32[8,320,128]{2,1,0:T(8,128)S(1)}, f32[8,320,128]{2,1,0:T(8,128)S(1)}, u32[]{:S(2)}, u32[]{:S(2)}) collective-permute-start(f32[8,320,128]{2,1,0:T(8,128)S(1)} %get-tuple-element.36), channel_id=1, source_target_pairs={{0,1},{1,0},{2,3},{3,2},{4,5},{5,4},{6,7},{7,6},{8,9},{9,8},{10,11... | collective-permute-start | bytes 3932168 | tf_op jit(solution)/shard_map/ppermute | solution.py:303
  61.1 12.1 %collective-permute-start.17 = (f32[2,320,128]{2,1,0:T(8,128)S(1)}, f32[2,320,128]{2,1,0:T(8,128)S(1)}, u32[]{:S(2)}, u32[]{:S(2)}) collective-permute-start(f32[2,320,128]{2,1,0:T(8,128)S(1)} %get-tuple-element.45), channel_id=1, source_target_pairs={{0,8},{1,9},{2,10},{3,11},{16,24},{17,25},{18,26},{19,27}} | collective-permute-start | bytes 983048 | tf_op jit(solution)/shard_map/ppermute | solution.py:303
  62.4 12.8 %collective-permute-start.18 = (f32[2,320,128]{2,1,0:T(8,128)S(1)}, f32[2,320,128]{2,1,0:T(8,128)S(1)}, u32[]{:S(2)}, u32[]{:S(2)}) collective-permute-start(f32[2,320,128]{2,1,0:T(8,128)S(1)} %get-tuple-element.46), channel_id=1, source_target_pairs={{0,12},{1,13},{2,14},{3,15},{16,28},{17,29},{18,30},{19,31}} | collective-permute-start | bytes 983048 | tf_op jit(solution)/shard_map/ppermute | solution.py:303
  63.1 12.1 %collective-permute-start.16 = (f32[2,320,128]{2,1,0:T(8,128)S(1)}, f32[2,320,128]{2,1,0:T(8,128)S(1)}, u32[]{:S(2)}, u32[]{:S(2)}) collective-permute-start(f32[2,320,128]{2,1,0:T(8,128)S(1)} %get-tuple-element.47), channel_id=1, source_target_pairs={{0,4},{1,5},{2,6},{3,7},{16,20},{17,21},{18,22},{19,23}} | collective-permute-start | bytes 983048 | tf_op jit(solution)/shard_map/ppermute | solution.py:303
  63.8 17.1 %collective-permute-start.1 = (f32[4,320,128]{2,1,0:T(8,128)S(1)}, f32[4,320,128]{2,1,0:T(8,128)S(1)}, u32[]{:S(2)}, u32[]{:S(2)}) collective-permute-start(f32[4,320,128]{2,1,0:T(8,128)S(1)} %slice_add_fusion.2), channel_id=1, source_target_pairs={{0,2},{1,3},{2,0},{3,1},{4,6},{5,7},{6,4},{7,5},{8,10},{9,11},{10,... | collective-permute-start | bytes 1966088 | tf_op jit(solution)/shard_map/ppermute | solution.py:303
  69.3 25.8 %collective-permute-start.11 = (f32[8,320,128]{2,1,0:T(8,128)S(1)}, f32[8,320,128]{2,1,0:T(8,128)S(1)}, u32[]{:S(2)}, u32[]{:S(2)}) collective-permute-start(f32[8,320,128]{2,1,0:T(8,128)S(1)} %get-tuple-element.40), channel_id=1, source_target_pairs={{0,1},{1,0},{2,3},{3,2},{4,5},{5,4},{6,7},{7,6},{8,9},{9,8},{10,11... | collective-permute-start | bytes 3932168 | tf_op jit(solution)/shard_map/ppermute | solution.py:303
  73.2 21.9 %collective-permute-start.6 = (f32[4,320,128]{2,1,0:T(8,128)S(1)}, f32[4,320,128]{2,1,0:T(8,128)S(1)}, u32[]{:S(2)}, u32[]{:S(2)}) collective-permute-start(f32[4,320,128]{2,1,0:T(8,128)S(1)} %slice_add_fusion), channel_id=1, source_target_pairs={{0,2},{1,3},{2,0},{3,1},{4,6},{5,7},{6,4},{7,5},{8,10},{9,11},{10,... | collective-permute-start | bytes 1966088 | tf_op jit(solution)/shard_map/ppermute | solution.py:303
  81.1 21.3 %collective-permute-start.4 = (f32[320,128]{1,0:T(8,128)S(1)}, f32[320,128]{1,0:T(8,128)S(1)}, u32[]{:S(2)}, u32[]{:S(2)}) collective-permute-start(f32[320,128]{1,0:T(8,128)S(1)} %get-tuple-element.56), channel_id=1, source_target_pairs={{0,12},{1,13},{2,14},{3,15},{4,8},{5,9},{6,10},{7,11},{8,4},{9,5},... | collective-permute-start | bytes 491528 | tf_op jit(solution)/shard_map/ppermute | solution.py:303
  87.8 16.5 %collective-permute-start.3 = (f32[320,128]{1,0:T(8,128)S(1)}, f32[320,128]{1,0:T(8,128)S(1)}, u32[]{:S(2)}, u32[]{:S(2)}) collective-permute-start(f32[320,128]{1,0:T(8,128)S(1)} %get-tuple-element.57), channel_id=1, source_target_pairs={{0,8},{1,9},{2,10},{3,11},{4,12},{5,13},{6,14},{7,15},{8,0},{9,1},... | collective-permute-start | bytes 491528 | tf_op jit(solution)/shard_map/ppermute | solution.py:303
  87.8 17.9 %collective-permute-start.2 = (f32[320,128]{1,0:T(8,128)S(1)}, f32[320,128]{1,0:T(8,128)S(1)}, u32[]{:S(2)}, u32[]{:S(2)}) collective-permute-start(f32[320,128]{1,0:T(8,128)S(1)} %get-tuple-element.58), channel_id=1, source_target_pairs={{0,4},{1,5},{2,6},{3,7},{4,0},{5,1},{6,2},{7,3},{8,12},{9,13},{10,... | collective-permute-start | bytes 491528 | tf_op jit(solution)/shard_map/ppermute | solution.py:303
  95.2 23.0 %collective-permute-start.12 = (f32[4,320,128]{2,1,0:T(8,128)S(1)}, f32[4,320,128]{2,1,0:T(8,128)S(1)}, u32[]{:S(2)}, u32[]{:S(2)}) collective-permute-start(f32[4,320,128]{2,1,0:T(8,128)S(1)} %slice_add_fusion.4), channel_id=1, source_target_pairs={{0,2},{1,3},{2,0},{3,1},{4,6},{5,7},{6,4},{7,5},{8,10},{9,11},{10,... | collective-permute-start | bytes 1966088 | tf_op jit(solution)/shard_map/ppermute | solution.py:303
  96.6 9.2 %collective-permute-start.8 = (f32[320,128]{1,0:T(8,128)S(1)}, f32[320,128]{1,0:T(8,128)S(1)}, u32[]{:S(2)}, u32[]{:S(2)}) collective-permute-start(f32[320,128]{1,0:T(8,128)S(1)} %get-tuple-element.50), channel_id=1, source_target_pairs={{0,8},{1,9},{2,10},{3,11},{4,12},{5,13},{6,14},{7,15},{8,0},{9,1},... | collective-permute-start | bytes 491528 | tf_op jit(solution)/shard_map/ppermute | solution.py:303
  102.4 13.7 %collective-permute-start.9 = (f32[320,128]{1,0:T(8,128)S(1)}, f32[320,128]{1,0:T(8,128)S(1)}, u32[]{:S(2)}, u32[]{:S(2)}) collective-permute-start(f32[320,128]{1,0:T(8,128)S(1)} %get-tuple-element.51), channel_id=1, source_target_pairs={{0,12},{1,13},{2,14},{3,15},{4,8},{5,9},{6,10},{7,11},{8,4},{9,5},... | collective-permute-start | bytes 491528 | tf_op jit(solution)/shard_map/ppermute | solution.py:303
  104.4 11.7 %collective-permute-start.7 = (f32[320,128]{1,0:T(8,128)S(1)}, f32[320,128]{1,0:T(8,128)S(1)}, u32[]{:S(2)}, u32[]{:S(2)}) collective-permute-start(f32[320,128]{1,0:T(8,128)S(1)} %get-tuple-element.52), channel_id=1, source_target_pairs={{0,4},{1,5},{2,6},{3,7},{4,0},{5,1},{6,2},{7,3},{8,12},{9,13},{10,... | collective-permute-start | bytes 491528 | tf_op jit(solution)/shard_map/ppermute | solution.py:303
  116.1 6.2 %collective-permute-start.19 = (f32[320,128]{1,0:T(8,128)S(1)}, f32[320,128]{1,0:T(8,128)S(1)}, u32[]{:S(2)}, u32[]{:S(2)}) collective-permute-start(f32[320,128]{1,0:T(8,128)S(1)} %slice_bitcast_fusion.4), channel_id=1, source_target_pairs={{0,2},{1,3},{2,0},{3,1},{4,6},{5,7},{6,4},{7,5},{8,10},{9,11},{10,... | collective-permute-start | bytes 491528 | tf_op jit(solution)/shard_map/ppermute | solution.py:303
  118.3 19.8 %copy-start.5 = (bf16[1280,640]{1,0:T(8,128)(2,1)S(1)}, bf16[1280,640]{1,0:T(8,128)(2,1)}, u32[]{:S(2)}) copy-start(bf16[1280,640]{1,0:T(8,128)(2,1)} %copy-done.4) | copy-start | bytes 4915204
  118.3 7.9 %collective-permute-start.14 = (f32[320,128]{1,0:T(8,128)S(1)}, f32[320,128]{1,0:T(8,128)S(1)}, u32[]{:S(2)}, u32[]{:S(2)}) collective-permute-start(f32[320,128]{1,0:T(8,128)S(1)} %get-tuple-element.53), channel_id=1, source_target_pairs={{0,8},{1,9},{2,10},{3,11},{4,12},{5,13},{6,14},{7,15},{16,24},{17,... | collective-permute-start | bytes 491528 | tf_op jit(solution)/shard_map/ppermute | solution.py:303
  119.8 18.1 %collective-permute-start.15 = (f32[320,128]{1,0:T(8,128)S(1)}, f32[320,128]{1,0:T(8,128)S(1)}, u32[]{:S(2)}, u32[]{:S(2)}) collective-permute-start(f32[320,128]{1,0:T(8,128)S(1)} %get-tuple-element.54), channel_id=1, source_target_pairs={{0,12},{1,13},{2,14},{3,15},{4,8},{5,9},{6,10},{7,11},{16,28},{17,... | collective-permute-start | bytes 491528 | tf_op jit(solution)/shard_map/ppermute | solution.py:303
  121.1 17.0 %copy-start.3 = (bf16[1280,640]{1,0:T(8,128)(2,1)S(1)}, bf16[1280,640]{1,0:T(8,128)(2,1)}, u32[]{:S(2)}) copy-start(bf16[1280,640]{1,0:T(8,128)(2,1)} %copy-done.2) | copy-start | bytes 4915204
  121.1 17.0 %copy-start.7 = (f32[128]{0:T(128)S(1)}, f32[128]{0:T(128)}, u32[]{:S(2)}) copy-start(f32[128]{0:T(128)} %param.11) | copy-start | bytes 1540
  121.1 16.8 %collective-permute-start.13 = (f32[320,128]{1,0:T(8,128)S(1)}, f32[320,128]{1,0:T(8,128)S(1)}, u32[]{:S(2)}, u32[]{:S(2)}) collective-permute-start(f32[320,128]{1,0:T(8,128)S(1)} %get-tuple-element.55), channel_id=1, source_target_pairs={{0,4},{1,5},{2,6},{3,7},{4,0},{5,1},{6,2},{7,3},{16,20},{17,21},{1... | collective-permute-start | bytes 491528 | tf_op jit(solution)/shard_map/ppermute | solution.py:303
  (8 other events, 20.3 us)

commit v3 on v2

--- a/solution.py
+++ b/solution.py
@@ -11,6 +11,7 @@
 NLON = 1280
 STEP = 32
 PLANES = 4
+HALVES = 1
 LANES = 128
 
 PRECISE = lax.Precision.HIGHEST
@@ -99,8 +100,10 @@
     held, _, slots, rows = legendre.shape
     groups, own = held // 4, slots // spec
     lanes = rows * 8
-
-    def body(me_ref, leg_ref, out_ref, turned):
+    share = groups // HALVES
+
+    def body(me_ref, leg_ref, *refs):
+        turned = refs[-1]
         pair = lax.broadcasted_iota(jnp.int32, (8, slots), 0)
         slot = lax.broadcasted_iota(jnp.int32, (8, slots), 1)
         for group in range(groups):
@@ -113,7 +116,8 @@
             turned[...] = block.T
             for goal in range(spec):
                 piece = turned[goal * own:(goal + 1) * own, :]
-                out_ref[goal, group * own:(group + 1) * own, :] = piece
+                at = group % share
+                refs[group // share][goal, at * own:(at + 1) * own, :] = piece
 
     return pl.pallas_call(
         body,
@@ -121,19 +125,18 @@
             num_scalar_prefetch=1,
             grid=(1,),
             in_specs=[pl.BlockSpec((held, 2, rows, slots), lambda i, f: (0, 0, 0, 0))],
-            out_specs=pl.BlockSpec((spec, groups * own, lanes), lambda i, f: (0, 0, 0)),
+            out_specs=[pl.BlockSpec((spec, share * own, lanes), lambda i, f: (0, 0, 0))] * HALVES,
             scratch_shapes=[pltpu.VMEM((slots, lanes), F32)],
         ),
-        out_shape=jax.ShapeDtypeStruct((spec, groups * own, lanes), F32),
+        out_shape=[jax.ShapeDtypeStruct((spec, share * own, lanes), F32)] * HALVES,
         compiler_params=pltpu.CompilerParams(vmem_limit_bytes=32 << 20),
         cost_estimate=pl.CostEstimate(flops=1, bytes_accessed=1, transcendentals=0),
         name="arrange_legendre",
     )(me[None], jnp.transpose(legendre, (0, 1, 3, 2)))
 
 
-def partial_rows(order, arranged, coefficients, plane, own):
-    spec, depth, lanes = arranged.shape
-    sources = spec // PLANES
+def partial_rows(order, arranged, coefficients, first, sources, half_at, own):
+    _, depth, lanes = arranged.shape
     groups = depth // own
     half = lanes // 16
     columns = coefficients.shape[-1]
@@ -167,8 +170,8 @@
             num_scalar_prefetch=1,
             grid=(sources,),
             in_specs=[
-                pl.BlockSpec((1, depth, lanes), lambda i, o: (plane * sources + i, 0, 0)),
-                pl.BlockSpec((groups * span, columns), lambda i, o: (plane * sources + i, 0)),
+                pl.BlockSpec((1, depth, lanes), lambda i, o: (first + i, 0, 0)),
+                pl.BlockSpec((groups * span, columns), lambda i, o: (HALVES * (first + i) + half_at, 0)),
             ],
             out_specs=[out_spec, out_spec],
             scratch_shapes=[pltpu.VMEM((span, lanes), F32)],
@@ -180,114 +183,147 @@
     )(order, arranged, coefficients)
 
 
-def wave_tables(row_count, waves):
-    orders = jnp.arange(waves, dtype=jnp.int32)
-    weights = jnp.where(orders == 0, 1.0, 2.0) * (2 * orders < row_count).astype(F32)
+def wave_tables(row_count, orders):
     steps = NLON // STEP
     coarse = STEP * jnp.arange(steps, dtype=jnp.int32)
-    places = jnp.concatenate((coarse, jnp.arange(STEP, dtype=jnp.int32)))
-    phases = places[:, None] * orders[None, :] % row_count
-    angles = 2.0 * math.pi * phases.astype(F32) / row_count.astype(F32)
-    gain = jnp.where(jnp.arange(places.shape[0])[:, None] < steps, weights[None, :], 1.0)
-    bases = (gain * jnp.cos(angles), gain * jnp.sin(angles))
+    places = jnp.concatenate((coarse, jnp.arange(STEP, dtype=jnp.int32)))[:, None]
+    bases = []
+    for order in orders:
+        weights = jnp.where(order == 0, 1.0, 2.0) * (2 * order < row_count).astype(F32)
+        angles = 2.0 * math.pi * (places * order[None, :] % row_count).astype(F32) / row_count.astype(F32)
+        gain = jnp.where(jnp.arange(places.shape[0])[:, None] < steps, weights[None, :], 1.0)
+        bases += [gain * jnp.cos(angles), gain * jnp.sin(angles)]
     parts = 8
 
-    def body(cos_ref, sin_ref, ch_ref, cl_ref, sh_ref, sl_ref):
-        cos_fine, sin_fine = cos_ref[steps:, :], sin_ref[steps:, :]
-        for part in range(parts):
-            at = pl.program_id(0) * parts + part
-            cos_at, sin_at = cos_ref[pl.ds(at, 1), :], sin_ref[pl.ds(at, 1), :]
-            here = slice(part * STEP, (part + 1) * STEP)
-            ch_ref[here, :], cl_ref[here, :] = split_pair(cos_at * cos_fine - sin_at * sin_fine)
-            sh_ref[here, :], sl_ref[here, :] = split_pair(sin_at * cos_fine + cos_at * sin_fine)
+    def body(*refs):
+        for at in range(0, len(bases), 2):
+            cos_ref, sin_ref = refs[at], refs[at + 1]
+            cos_fine, sin_fine = cos_ref[steps:, :], sin_ref[steps:, :]
+            for part in range(parts):
+                step = pl.program_id(0) * parts + part
+                here = slice(part * STEP, (part + 1) * STEP)
+                cos_at, sin_at = cos_ref[pl.ds(step, 1), :], sin_ref[pl.ds(step, 1), :]
+                both = (cos_at * cos_fine - sin_at * sin_fine, sin_at * cos_fine + cos_at * sin_fine)
+                for kind in range(2):
+                    high, low = split_pair(both[kind])
+                    refs[len(bases) + at + kind][here, :] = jnp.concatenate([high, low, high], axis=1)
 
     tile = parts * STEP
     return pl.pallas_call(
         body,
         grid=(NLON // tile,),
-        in_specs=[pl.BlockSpec(bases[0].shape, lambda i: (0, 0))] * 2,
-        out_specs=[pl.BlockSpec((tile, waves), lambda i: (i, 0))] * 4,
-        out_shape=[jax.ShapeDtypeStruct((NLON, waves), BF16)] * 4,
+        in_specs=[pl.BlockSpec(base.shape, lambda i: (0, 0)) for base in bases],
+        out_specs=[pl.BlockSpec((tile, 3 * base.shape[1]), lambda i: (i, 0)) for base in bases],
+        out_shape=[jax.ShapeDtypeStruct((NLON, 3 * base.shape[1]), BF16) for base in bases],
         compiler_params=pltpu.CompilerParams(vmem_limit_bytes=32 << 20),
         cost_estimate=pl.CostEstimate(flops=1, bytes_accessed=1, transcendentals=0),
         name="wave_tables",
     )(*bases)
 
 
-def synthesize(scalars, spectra, tables, basis, absorb, kernel):
-    planes, deep, columns = spectra.shape
-    span = deep // 2
-    waves = planes * span
+def stack_spectra(spec_ref, stack_ref):
+    waves, columns = spec_ref.shape[0] // 2, spec_ref.shape[1]
+    for parity in range(2):
+        high, low = split_pair(spec_ref[pl.ds(parity, waves, stride=2), :])
+        here = slice(parity * columns, (parity + 1) * columns)
+        stack_ref[:waves, here] = high
+        stack_ref[waves:2 * waves, here] = high
+        stack_ref[2 * waves:, here] = low
+
+
+def fourier_sums(spectra, tables):
+    deep, columns = spectra.shape
+    depth = deep // 2 * 3
+    tile = 8 * STEP
+
+    def body(spec_ref, cos_ref, sin_ref, out_ref, stack_ref):
+        @pl.when(pl.program_id(0) == 0)
+        def _():
+            stack_spectra(spec_ref, stack_ref)
+
+        for kind, table_ref in enumerate((cos_ref, sin_ref)):
+            here = slice(2 * kind * columns, 2 * (kind + 1) * columns)
+            out_ref[:, here] = jnp.dot(table_ref[...], stack_ref[...], preferred_element_type=F32)
+
+    return pl.pallas_call(
+        body,
+        grid=(NLON // tile,),
+        in_specs=[pl.BlockSpec((deep, columns), lambda i: (0, 0))]
+        + [pl.BlockSpec((tile, depth), lambda i: (i, 0))] * 2,
+        out_specs=pl.BlockSpec((tile, 4 * columns), lambda i: (i, 0)),
+        out_shape=jax.ShapeDtypeStruct((NLON, 4 * columns), F32),
+        scratch_shapes=[pltpu.VMEM((depth, 2 * columns), BF16)],
+        compiler_params=pltpu.CompilerParams(vmem_limit_bytes=32 << 20),
+        cost_estimate=pl.CostEstimate(flops=1, bytes_accessed=1, transcendentals=0),
+        name="fourier_sums",
+    )(spectra, *tables)
+
+
+def synthesize(row_counts, first_sums, spectra, tables, basis, absorb, kernel_high, kernel_low):
+    deep, columns = spectra.shape
+    depth = deep // 2 * 3
     levels = basis.shape[1]
-    channels = kernel.shape[1]
+    channels = kernel_high.shape[1]
     tile = 8 * STEP
     zero = jnp.zeros_like(basis)
     widened = jnp.concatenate((basis, zero, zero, -basis), axis=0)
     basis_high, basis_low = split_constant(widened)
-    kernel_high, kernel_low = split_constant(kernel)
-
-    def body(scalar_ref, spec_ref, ch_ref, cl_ref, sh_ref, sl_ref, bh_ref, bl_ref, ab_ref, kh_ref, kl_ref,
-             out_ref, high_ref, low_ref):
+    kernel_twice = jnp.concatenate((kernel_high, kernel_high), axis=0)
+
+    def body(count_ref, sums_ref, spec_ref, cos_ref, sin_ref, bh_ref, bl_ref, ab_ref, kh_ref, kl_ref, out_ref, stack_ref):
         step = pl.program_id(0)
 
         @pl.when(step == 0)
         def _():
-            for plane in range(planes):
-                here = pl.ds(pl.multiple_of(scalar_ref[1 + plane] * span, 16), span)
-                for parity in range(2):
-                    high, low = split_pair(spec_ref[plane, pl.ds(parity, span, stride=2), :])
-                    high_ref[here, parity * columns:(parity + 1) * columns] = high
-                    low_ref[here, parity * columns:(parity + 1) * columns] = low
+            stack_spectra(spec_ref, stack_ref)
 
         sides = []
-        for first_ref, second_ref in ((ch_ref, cl_ref), (sh_ref, sl_ref)):
-            fields = jnp.dot(first_ref[...], high_ref[...], preferred_element_type=F32)
-            fields += jnp.dot(second_ref[...], high_ref[...], preferred_element_type=F32)
-            fields += jnp.dot(first_ref[...], low_ref[...], preferred_element_type=F32)
+        for kind, table_ref in enumerate((cos_ref, sin_ref)):
+            fields = jnp.dot(table_ref[...], stack_ref[...], preferred_element_type=F32)
+            fields += sums_ref[:, 2 * kind * columns:2 * (kind + 1) * columns]
             even, odd = fields[:, :columns], fields[:, columns:]
             sides.append((even + odd, even - odd))
-        both = jnp.concatenate(
-            [jnp.concatenate([sides[0][side], sides[1][side]], axis=1) for side in range(2)], axis=0
-        )
-        high, low = split_pair(both)
-        temps = jnp.dot(high, bh_ref[...], preferred_element_type=F32)
-        temps += jnp.dot(low, bh_ref[...], preferred_element_type=F32)
-        temps += jnp.dot(high, bl_ref[...], preferred_element_type=F32)
-        source = jnp.exp(0.5 * temps)
-        layers = ab_ref[...] * source
-        above = lax.broadcasted_iota(jnp.int32, (2 * levels, levels), 0) % levels
-        level = lax.broadcasted_iota(jnp.int32, (2 * levels, levels), 1)
-        upper = jnp.where(above < level, 1.0, 0.0).astype(BF16)
-        overhead = jnp.dot(jnp.concatenate(split_pair(layers), axis=1), upper, preferred_element_type=F32)
-        half = jnp.tanh(0.5 * layers)
-        emitted = source * jnp.exp(-overhead) * (2.0 * half / (1.0 + half))
-        high, low = split_pair(emitted)
-        bright = jnp.dot(high, kh_ref[...], preferred_element_type=F32)
-        bright += jnp.dot(low, kh_ref[...], preferred_element_type=F32)
-        bright += jnp.dot(high, kl_ref[...], preferred_element_type=F32)
-        place = step * tile + lax.broadcasted_iota(jnp.int32, (2 * tile, 1), 0) % tile
-        bright = jnp.where(place < scalar_ref[0], bright, 0.0)
-        out_ref[0] = bright.reshape(2, tile, channels)
+        for side in range(2):
+            high, low = split_pair(jnp.concatenate([sides[0][side], sides[1][side]], axis=1))
+            temps = jnp.dot(high, bh_ref[...], preferred_element_type=F32)
+            temps += jnp.dot(low, bh_ref[...], preferred_element_type=F32)
+            temps += jnp.dot(high, bl_ref[...], preferred_element_type=F32)
+            source = jnp.exp(0.5 * temps)
+            layers = ab_ref[...] * source
+            above = lax.broadcasted_iota(jnp.int32, (2 * levels, levels), 0) % levels
+            level = lax.broadcasted_iota(jnp.int32, (2 * levels, levels), 1)
+            upper = jnp.where(above < level, 1.0, 0.0).astype(BF16)
+            overhead = jnp.dot(jnp.concatenate(split_pair(layers), axis=1), upper, preferred_element_type=F32)
+            half = jnp.tanh(0.5 * layers)
+            emitted = source * jnp.exp(-overhead) * (2.0 * half / (1.0 + half))
+            high, low = split_pair(emitted)
+            bright = jnp.dot(jnp.concatenate([high, low], axis=1), kh_ref[...], preferred_element_type=F32)
+            bright += jnp.dot(high, kl_ref[...], preferred_element_type=F32)
+            place = step * tile + lax.broadcasted_iota(jnp.int32, (tile, 1), 0)
+            out_ref[0, side] = jnp.where(place < count_ref[0], bright, 0.0)
 
     def whole(array):
         return pl.BlockSpec(array.shape, lambda i, c: (0,) * array.ndim)
 
-    constants = (basis_high, basis_low, absorb[None, :], kernel_high, kernel_low)
-    table_spec = pl.BlockSpec((tile, waves), lambda i, c: (i, 0))
+    def tiled(wide):
+        return pl.BlockSpec((tile, wide), lambda i, c: (i, 0))
+
+    constants = (basis_high, basis_low, absorb[None, :], kernel_twice, kernel_low)
     return pl.pallas_call(
         body,
         grid_spec=pltpu.PrefetchScalarGridSpec(
             num_scalar_prefetch=1,
             grid=(NLON // tile,),
-            in_specs=[whole(spectra)] + [table_spec] * 4 + [whole(array) for array in constants],
+            in_specs=[tiled(4 * columns), whole(spectra), tiled(depth), tiled(depth)]
+            + [whole(array) for array in constants],
             out_specs=pl.BlockSpec((1, 2, tile, channels), lambda i, c: (0, 0, i, 0)),
-            scratch_shapes=[pltpu.VMEM((waves, 2 * columns), BF16)] * 2,
+            scratch_shapes=[pltpu.VMEM((depth, 2 * columns), BF16)],
         ),
         out_shape=jax.ShapeDtypeStruct((1, 2, NLON, channels), F32),
         compiler_params=pltpu.CompilerParams(vmem_limit_bytes=48 << 20),
         cost_estimate=pl.CostEstimate(flops=1, bytes_accessed=1, transcendentals=0),
         name="synthesize",
-    )(scalars, spectra, *tables, *constants)
+    )(row_counts, first_sums, spectra, *tables, *constants)
 
 
 def move_legendre(spec, coefficients, legendre, row_counts, basis, absorb, peak_level, width):
@@ -306,15 +342,15 @@
         return lax.optimization_barrier((values, earlier))[0]
 
     arranged = arrange_legendre(legendre, me, spec, waves)
-    tables = wave_tables(row_counts[0], waves)
-    kernel = channel_kernel(peak_level, width, basis.shape[1])
-    arrived = lax.all_to_all(arranged, "spec", split_axis=0, concat_axis=0, tiled=True)
-    arrived = after(arrived, (tables, kernel))
+    arrived = [lax.all_to_all(half, "spec", split_axis=0, concat_axis=0, tiled=True) for half in arranged]
+    plane_waves = jnp.arange(waves, dtype=jnp.int32).reshape(PLANES, -1)
+    tables = wave_tables(row_counts[0], (jnp.concatenate((plane_waves[:2].reshape(-1), plane_waves[3])), plane_waves[2]))
+    kernel = split_constant(channel_kernel(peak_level, width, basis.shape[1]))
     couple = jnp.arange(spec // 2, dtype=jnp.int32) ^ (me >> 1)
     order = jnp.concatenate(((couple & 1) * quarter + (couple >> 1), (me & 1)[None]))
 
-    def contract(plane, earlier=()):
-        return partial_rows(after(order, earlier), arrived, natural, plane, own)
+    def contract(plane, earlier):
+        return partial_rows(after(order, earlier), arrived[0], natural, plane * sources, sources, 0, own)
 
     def add_cores(keep, other):
         return keep[quarter:] + other[quarter:], keep[:quarter] + other[:quarter]
@@ -323,28 +359,28 @@
         use = lambda i: (plane * held + 2 * (i // sources) * own) * sources < waves
         return [swap(value[away], sources * away, use) for away in range(1, PLANES)]
 
-    keep3, send3 = contract(3)
+    keep3, send3 = contract(3, (tables, kernel))
     keep0, send0 = contract(0, send3)
     keep1, send1 = contract(1, send0)
-    both3 = keep3 + swap(send3, 1)
-    early = between_planes(jnp.swapaxes(both3.reshape(2, quarter, *both3.shape[1:]), 0, 1), 3)
+    both3 = (keep3 + swap(send3, 1)).reshape(2, quarter, *keep3.shape[1:])
+    early = between_planes(jnp.swapaxes(both3, 0, 1), 3)
     side0, own0 = add_cores(keep0, swap(send0, 1))
     keep2, send2 = contract(2, (side0, both3, send1))
     sum0 = own0 + swap(side0, 2)
     side1, own1 = add_cores(keep1, swap(send1, 1))
-    late0 = between_planes(sum0, 0)
+    late0 = between_planes(after(sum0, early), 0)
 
     keep2, other2 = after((keep2, swap(send2, 1)), (sum0, side1))
     side2, own2 = add_cores(keep2, other2)
     sum1 = own1 + swap(side1, 2)
-    late1 = between_planes(sum1, 1)
-    sum3 = both3.reshape(2, quarter, *both3.shape[1:])[:, 0] + sum(early)
+    late1 = between_planes(after(sum1, side2), 1)
+    sum3 = both3[:, 0] + sum(early)
     sum3 = sum3[0] + swap(after(sum3[1], side2), 2)
     sum2 = own2 + swap(side2, 2)
-    late2 = between_planes(after(sum2, late0), 2)
-    spectra = jnp.stack([sum0[0] + sum(late0), sum1[0] + sum(late1), sum2[0] + sum(late2), sum3])
-    scalars = jnp.concatenate((row_counts, jnp.arange(PLANES, dtype=jnp.int32)))
-    return synthesize(scalars, spectra, tables, basis, absorb, kernel)
+    late2 = between_planes(after(sum2, (late0, late1, sum3)), 2)
+    first_sums = fourier_sums(jnp.concatenate((sum0[0] + sum(late0), sum1[0] + sum(late1), sum3)), tables[:2])
+    last = sum2[0] + sum(late2)
+    return synthesize(row_counts, first_sums, last, tables[2:], basis, absorb, *kernel)
 
 
 def solution(mesh):
@@ -362,7 +398,7 @@
     def on_device(coefficients, legendre, *others):
         held, _, _, rows = legendre.shape
         own = coefficients.shape[2]
-        if rows == spec and 8 * rows == LANES and held % 8 == 0 and rows <= own:
+        if rows == spec and 8 * rows == LANES and held % (4 * HALVES) == 0 and rows <= own:
             return move_legendre(spec, coefficients, legendre, *others)
         return move_coefficients(coefficients, legendre, *others)
 

time: 151 us -> 149 us (0.987)
  the two profiles are of different devices: /device:TPU:23 before, /device:TPU:0 now
where the time goes in v3:
time: 149 us; the launch traced here: 148 us
  waiting for transfers between devices  53.5 us (36%)
  starting transfers between devices  49.8 us (33%)
  Pallas kernels  29.3 us (20%)
  local copies, waits for them, and re-layouts  9.73 us (7%)
  other arithmetic  4.84 us (3%)
    ppermute x20, starting transfers between devices, swap(): return lax.ppermute(value, 'spec', pairs)  42.3 us
    ppermute x20, waiting for transfers between devices, swap(): return lax.ppermute(value, 'spec', pairs)  32.4 us
    all_to_all x1, waiting for transfers between devices, move_legendre(): lax.all_to_all(half, 'spec', split_axis=0, concat_axis=0, tiled=True)  21.1 us
    pallas_call x4, Pallas kernels, partial_rows(): pl.pallas_call(body, grid_spec=pltpu.PrefetchScalarGridSpec(num_scalar_pr...  13.5 us
    unnamed x24, local copies, waits for them, and re-layouts  9.29 us
    pallas_call x1, Pallas kernels, synthesize(): pl.pallas_call(body, grid_spec=pltpu.PrefetchScalarGridSpec(num_scalar_pr...  8.05 us
    all_to_all x1, starting transfers between devices, move_legendre(): lax.all_to_all(half, 'spec', split_axis=0, concat_axis=0, tiled=True)  7.52 us
    mul x2, other arithmetic, wave_tables(): bases += [gain * jnp.cos(angles), gain * jnp.sin(angles)]  3.17 us
  transfers between devices with their start and end apart: 21, of which 9 were waited for; matrix products, arithmetic and copies ran while one was open for 3% of the time, Pallas kernels for 11%

profile of v3, /device:TPU:0, one launch (start us, length us, event | category | flops | bytes accessed | tf_op | source)
XLA Modules:
  0.0 148.3 jit_solution(8940570498210171384)
XLA Ops:
  1.5 2.0 %arrange_legendre.1 = f32[16,200,128]{2,1,0:T(8,128)} custom-call(s32[1]{0:T(128)} %bitcast.5.me_ref, f32[40,2,16,320]{3,2,1,0:T(8,128)S(1)} %bitcast.70), custom_call_target="tpu_custom_call" | custom-call | flops 1 | bytes 1 | tf_op jit(solution)/shard_map/arrange_legendre/pallas_call | solution.py:122
  3.6 7.5 %all-to-all-start = ((f32[16,200,128]{2,1,0:T(8,128)}), f32[16,200,128]{2,1,0:T(8,128)S(1)}, u32[]{:S(2)}, u32[]{:S(2)}) async-start(f32[16,200,128]{2,1,0:T(8,128)} %arrange_legendre.1), calls=%async_computation | async-start | bytes 3276800 | tf_op jit(solution)/shard_map/all_to_all | solution.py:345
  13.1 2.1 %select_multiply_fusion = (f32[72,480]{1,0:T(8,128)S(1)}, f32[72,480]{1,0:T(8,128)S(1)}) fusion(f32[480]{0:T(512)S(1)} %get-tuple-element.49, pred[72]{0:T(512)(128)(4,1)S(1)} %iota_compare_fusion, f32[]{:T(128)S(6)} %convert_element_type.28, pred[]{:T(512)S(6)} %lt.46, s32[]{:T(128)S(6)} %select_n.38, s32[480]{0:T(512)S(1)} %get-tuple-element.50, ...), kind=kLoop, calls=%fused_computation.21 | loop fusion | flops 483840 | bytes 280689 | tf_op jit(solution)/shard_map/mul | solution.py:195
  15.2 2.7 %wave_tables.1 = (bf16[1280,1440]{1,0:T(8,128)(2,1)S(1)}, bf16[1280,1440]{1,0:T(8,128)(2,1)S(1)}, bf16[1280,480]{1,0:T(8,128)(2,1)S(1)}, bf16[1280,480]{1,0:T(8,128)(2,1)S(1)}) custom-call(f32[72,480]{1,0:T(8,128)S(1)} %get-tuple-element.70.refs_0_, f32[72,480]{1,0:T(8,128)S(1)} %get-tuple-element.69.refs_1_, f32[72,160]{1,0:T(8,128)S(1)} %get-tuple-element.74.refs_2_, ...), custom_call_target="tpu_custom_call" | custom-call | flops 1 | bytes 1 | tf_op jit(solution)/shard_map/wave_tables/pallas_call | solution.py:212
  23.1 21.1 %all-to-all-done.leg_ref = f32[16,200,128]{2,1,0:T(8,128)S(1)} async-done(((f32[16,200,128]{2,1,0:T(8,128)}), f32[16,200,128]{2,1,0:T(8,128)S(1)}, u32[]{:S(2)}, u32[]{:S(2)}) %all-to-all-start) | async-done | bytes 1638432 | tf_op jit(solution)/shard_map/all_to_all | solution.py:345
  44.2 2.9 %copy-done = bf16[640,2,20,128]{3,1,2,0:T(2,128)(2,1)S(1)} copy-done((bf16[640,2,20,128]{3,1,2,0:T(2,128)(2,1)S(1)}, bf16[640,2,20,128]{3,1,2,0:T(2,128)(2,1)}, u32[]{:S(2)}) %copy-start) | copy-done | bytes 6553624
  47.1 3.4 %partial_rows.4 = (f32[8,320,128]{2,1,0:T(8,128)S(1)}, f32[8,320,128]{2,1,0:T(8,128)S(1)}) custom-call(s32[9]{0:T(128)S(1)} %pad_add_fusion.1.order_ref, f32[16,200,128]{2,1,0:T(8,128)S(1)} %all-to-all-done.leg_ref, bf16[25600,128]{1,0:T(8,128)(2,1)S(1)} %bitcast.66), custom_call_target="tpu_custom_call" | custom-call | flops 1 | bytes 1 | tf_op jit(solution)/shard_map/partial_rows/pallas_call | solution.py:167
  51.3 3.4 %partial_rows.5 = (f32[8,320,128]{2,1,0:T(8,128)S(1)}, f32[8,320,128]{2,1,0:T(8,128)S(1)}) custom-call(s32[9]{0:T(128)S(1)} %pad_add_fusion.1.order_ref, f32[16,200,128]{2,1,0:T(8,128)S(1)} %all-to-all-done.leg_ref, bf16[25600,128]{1,0:T(8,128)(2,1)S(1)} %bitcast.67), custom_call_target="tpu_custom_call" | custom-call | flops 1 | bytes 1 | tf_op jit(solution)/shard_map/partial_rows/pallas_call | solution.py:167
  54.8 3.4 %partial_rows.6 = (f32[8,320,128]{2,1,0:T(8,128)S(1)}, f32[8,320,128]{2,1,0:T(8,128)S(1)}) custom-call(s32[9]{0:T(128)S(1)} %pad_add_fusion.1.order_ref, f32[16,200,128]{2,1,0:T(8,128)S(1)} %all-to-all-done.leg_ref, bf16[25600,128]{1,0:T(8,128)(2,1)S(1)} %bitcast.68), custom_call_target="tpu_custom_call" | custom-call | flops 1 | bytes 1 | tf_op jit(solution)/shard_map/partial_rows/pallas_call | solution.py:167
  59.2 8.8 %collective-permute-start.4 = (f32[2,320,128]{2,1,0:T(8,128)S(1)}, f32[2,320,128]{2,1,0:T(8,128)S(1)}, u32[]{:S(2)}, u32[]{:S(2)}) collective-permute-start(f32[2,320,128]{2,1,0:T(8,128)S(1)} %get-tuple-element.51), channel_id=1, source_target_pairs={{0,8},{1,9},{2,10},{3,11},{16,24},{17,25},{18,26},{19,27}} | collective-permute-start | bytes 983048 | tf_op jit(solution)/shard_map/ppermute | solution.py:339
  71.5 3.4 %partial_rows.7 = (f32[8,320,128]{2,1,0:T(8,128)S(1)}, f32[8,320,128]{2,1,0:T(8,128)S(1)}) custom-call(s32[9]{0:T(128)S(1)} %pad_add_fusion.1.order_ref, f32[16,200,128]{2,1,0:T(8,128)S(1)} %all-to-all-done.leg_ref, bf16[25600,128]{1,0:T(8,128)(2,1)S(1)} %bitcast.69), custom_call_target="tpu_custom_call" | custom-call | flops 1 | bytes 1 | tf_op jit(solution)/shard_map/partial_rows/pallas_call | solution.py:167
  76.5 6.5 %collective-permute-done.5 = f32[2,320,128]{2,1,0:T(8,128)S(1)} collective-permute-done((f32[2,320,128]{2,1,0:T(8,128)S(1)}, f32[2,320,128]{2,1,0:T(8,128)S(1)}, u32[]{:S(2)}, u32[]{:S(2)}) %collective-permute-start.5) | collective-permute-done | bytes 327712 | tf_op jit(solution)/shard_map/ppermute | solution.py:339
  83.0 6.6 %collective-permute-done.3 = f32[2,320,128]{2,1,0:T(8,128)S(1)} collective-permute-done((f32[2,320,128]{2,1,0:T(8,128)S(1)}, f32[2,320,128]{2,1,0:T(8,128)S(1)}, u32[]{:S(2)}, u32[]{:S(2)}) %collective-permute-start.3) | collective-permute-done | bytes 327712 | tf_op jit(solution)/shard_map/ppermute | solution.py:339
  90.0 4.8 %collective-permute-start.8 = (f32[320,128]{1,0:T(8,128)S(1)}, f32[320,128]{1,0:T(8,128)S(1)}, u32[]{:S(2)}, u32[]{:S(2)}) collective-permute-start(f32[320,128]{1,0:T(8,128)S(1)} %get-tuple-element.60), channel_id=1, source_target_pairs={{0,12},{1,13},{2,14},{3,15},{4,8},{5,9},{6,10},{7,11},{8,4},{9,5},... | collective-permute-start | bytes 491528 | tf_op jit(solution)/shard_map/ppermute | solution.py:339
  94.8 6.9 %collective-permute-done.10 = f32[4,320,128]{2,1,0:T(8,128)S(1)} collective-permute-done((f32[4,320,128]{2,1,0:T(8,128)S(1)}, f32[4,320,128]{2,1,0:T(8,128)S(1)}, u32[]{:S(2)}, u32[]{:S(2)}) %collective-permute-start.10) | collective-permute-done | bytes 655392 | tf_op jit(solution)/shard_map/ppermute | solution.py:339
  101.8 3.2 %collective-permute-done.7 = f32[320,128]{1,0:T(8,128)S(1)} collective-permute-done((f32[320,128]{1,0:T(8,128)S(1)}, f32[320,128]{1,0:T(8,128)S(1)}, u32[]{:S(2)}, u32[]{:S(2)}) %collective-permute-start.7) | collective-permute-done | bytes 163872 | tf_op jit(solution)/shard_map/ppermute | solution.py:339
  105.3 2.0 %collective-permute-start.15 = (f32[320,128]{1,0:T(8,128)S(1)}, f32[320,128]{1,0:T(8,128)S(1)}, u32[]{:S(2)}, u32[]{:S(2)}) collective-permute-start(f32[320,128]{1,0:T(8,128)S(1)} %slice_bitcast_fusion.5), channel_id=1, source_target_pairs={{0,2},{1,3},{2,0},{3,1},{4,6},{5,7},{6,4},{7,5},{8,10},{9,11},{10,... | collective-permute-start | bytes 491528 | tf_op jit(solution)/shard_map/ppermute | solution.py:339
  107.3 4.4 %collective-permute-start.13 = (f32[320,128]{1,0:T(8,128)S(1)}, f32[320,128]{1,0:T(8,128)S(1)}, u32[]{:S(2)}, u32[]{:S(2)}) collective-permute-start(f32[320,128]{1,0:T(8,128)S(1)} %get-tuple-element.62), channel_id=1, source_target_pairs={{0,8},{1,9},{2,10},{3,11},{4,12},{5,13},{6,14},{7,15},{8,0},{9,1},... | collective-permute-start | bytes 491528 | tf_op jit(solution)/shard_map/ppermute | solution.py:339
  113.0 3.5 %collective-permute-start.12 = (f32[320,128]{1,0:T(8,128)S(1)}, f32[320,128]{1,0:T(8,128)S(1)}, u32[]{:S(2)}, u32[]{:S(2)}) collective-permute-start(f32[320,128]{1,0:T(8,128)S(1)} %get-tuple-element.64), channel_id=1, source_target_pairs={{0,4},{1,5},{2,6},{3,7},{4,0},{5,1},{6,2},{7,3},{8,12},{9,13},{10,... | collective-permute-start | bytes 491528 | tf_op jit(solution)/shard_map/ppermute | solution.py:339
  116.6 5.3 %collective-permute-done.15 = f32[320,128]{1,0:T(8,128)S(1)} collective-permute-done((f32[320,128]{1,0:T(8,128)S(1)}, f32[320,128]{1,0:T(8,128)S(1)}, u32[]{:S(2)}, u32[]{:S(2)}) %collective-permute-start.15) | collective-permute-done | bytes 163872 | tf_op jit(solution)/shard_map/ppermute | solution.py:339
  122.2 8.2 %collective-permute-start.18 = (f32[320,128]{1,0:T(8,128)S(1)}, f32[320,128]{1,0:T(8,128)S(1)}, u32[]{:S(2)}, u32[]{:S(2)}) collective-permute-start(f32[320,128]{1,0:T(8,128)S(1)} %get-tuple-element.56), channel_id=1, source_target_pairs={{0,8},{1,9},{2,10},{3,11},{4,12},{5,13},{6,14},{7,15},{16,24},{17,... | collective-permute-start | bytes 491528 | tf_op jit(solution)/shard_map/ppermute | solution.py:339
  131.7 2.5 %collective-permute-start.17 = (f32[320,128]{1,0:T(8,128)S(1)}, f32[320,128]{1,0:T(8,128)S(1)}, u32[]{:S(2)}, u32[]{:S(2)}) collective-permute-start(f32[320,128]{1,0:T(8,128)S(1)} %get-tuple-element.58), channel_id=1, source_target_pairs={{0,4},{1,5},{2,6},{3,7},{4,0},{5,1},{6,2},{7,3},{16,20},{17,21},{1... | collective-permute-start | bytes 491528 | tf_op jit(solution)/shard_map/ppermute | solution.py:339
  134.3 3.0 %fourier_sums.1.sums_ref = f32[1280,512]{1,0:T(8,128)S(1)} custom-call(f32[960,128]{1,0:T(8,128)S(1)} %pad_maximum_fusion.spec_ref, bf16[1280,1440]{1,0:T(8,128)(2,1)S(1)} %copy-done.2, bf16[1280,1440]{1,0:T(8,128)(2,1)S(1)} %copy-done.4), custom_call_target="tpu_custom_call" | custom-call | flops 1 | bytes 1 | tf_op jit(solution)/shard_map/fourier_sums/pallas_call | solution.py:248
  140.3 8.0 %synthesize.1 = f32[1,2,1280,512]{3,2,1,0:T(8,128)} custom-call(s32[1]{0:T(128)} %copy.13.count_ref, f32[1280,512]{1,0:T(8,128)S(1)} %fourier_sums.1.sums_ref, f32[320,128]{1,0:T(8,128)S(1)} %fusion.7.spec_ref, bf16[1280,480]{1,0:T(8,128)(2,1)S(1)} %get-tuple-element.29.cos_ref, bf16[1280,480]{1,0:T(8,128)(2,1)S(1)} %copy-done.7, ...), custom_call_target="tpu_custom_call" | custom-call | flops 1 | bytes 1 | tf_op jit(solution)/shard_map/synthesize/pallas_call | solution.py:312
  (91 shorter events, 21.6 us)
Async XLA Ops:
  3.5 19.2 %copy-start.11 = (s32[512]{0:T(512)S(1)}, s32[512]{0:T(512)}, u32[]{:S(2)}) copy-start(s32[512]{0:T(512)} %param.12) | copy-start | bytes 6148
  3.5 19.3 %copy-start.10 = (f32[512]{0:T(512)S(1)}, f32[512]{0:T(512)}, u32[]{:S(2)}) copy-start(f32[512]{0:T(512)} %param.13) | copy-start | bytes 6148
  3.6 40.6 %all-to-all-start = ((f32[16,200,128]{2,1,0:T(8,128)}), f32[16,200,128]{2,1,0:T(8,128)S(1)}, u32[]{:S(2)}, u32[]{:S(2)}) async-start(f32[16,200,128]{2,1,0:T(8,128)} %arrange_legendre.1), calls=%async_computation | async-start | bytes 3276800 | tf_op jit(solution)/shard_map/all_to_all | solution.py:345
  50.5 8.4 %collective-permute-start.2 = (f32[8,320,128]{2,1,0:T(8,128)S(1)}, f32[8,320,128]{2,1,0:T(8,128)S(1)}, u32[]{:S(2)}, u32[]{:S(2)}) collective-permute-start(f32[8,320,128]{2,1,0:T(8,128)S(1)} %get-tuple-element.32), channel_id=1, source_target_pairs={{0,1},{1,0},{2,3},{3,2},{4,5},{5,4},{6,7},{7,6},{8,9},{9,8},{10,11... | collective-permute-start | bytes 3932168 | tf_op jit(solution)/shard_map/ppermute | solution.py:339
  54.7 16.0 %collective-permute-start = (f32[8,320,128]{2,1,0:T(8,128)S(1)}, f32[8,320,128]{2,1,0:T(8,128)S(1)}, u32[]{:S(2)}, u32[]{:S(2)}) collective-permute-start(f32[8,320,128]{2,1,0:T(8,128)S(1)} %get-tuple-element.35), channel_id=1, source_target_pairs={{0,1},{1,0},{2,3},{3,2},{4,5},{5,4},{6,7},{7,6},{8,9},{9,8},{10,11... | collective-permute-start | bytes 3932168 | tf_op jit(solution)/shard_map/ppermute | solution.py:339
  58.1 16.7 %collective-permute-start.9 = (f32[8,320,128]{2,1,0:T(8,128)S(1)}, f32[8,320,128]{2,1,0:T(8,128)S(1)}, u32[]{:S(2)}, u32[]{:S(2)}) collective-permute-start(f32[8,320,128]{2,1,0:T(8,128)S(1)} %get-tuple-element.40), channel_id=1, source_target_pairs={{0,1},{1,0},{2,3},{3,2},{4,5},{5,4},{6,7},{7,6},{8,9},{9,8},{10,11... | collective-permute-start | bytes 3932168 | tf_op jit(solution)/shard_map/ppermute | solution.py:339
  59.2 16.8 %collective-permute-start.4 = (f32[2,320,128]{2,1,0:T(8,128)S(1)}, f32[2,320,128]{2,1,0:T(8,128)S(1)}, u32[]{:S(2)}, u32[]{:S(2)}) collective-permute-start(f32[2,320,128]{2,1,0:T(8,128)S(1)} %get-tuple-element.51), channel_id=1, source_target_pairs={{0,8},{1,9},{2,10},{3,11},{16,24},{17,25},{18,26},{19,27}} | collective-permute-start | bytes 983048 | tf_op jit(solution)/shard_map/ppermute | solution.py:339
  68.0 15.0 %collective-permute-start.5 = (f32[2,320,128]{2,1,0:T(8,128)S(1)}, f32[2,320,128]{2,1,0:T(8,128)S(1)}, u32[]{:S(2)}, u32[]{:S(2)}) collective-permute-start(f32[2,320,128]{2,1,0:T(8,128)S(1)} %get-tuple-element.52), channel_id=1, source_target_pairs={{0,12},{1,13},{2,14},{3,15},{16,28},{17,29},{18,30},{19,31}} | collective-permute-start | bytes 983048 | tf_op jit(solution)/shard_map/ppermute | solution.py:339
  69.3 20.3 %collective-permute-start.3 = (f32[2,320,128]{2,1,0:T(8,128)S(1)}, f32[2,320,128]{2,1,0:T(8,128)S(1)}, u32[]{:S(2)}, u32[]{:S(2)}) collective-permute-start(f32[2,320,128]{2,1,0:T(8,128)S(1)} %get-tuple-element.53), channel_id=1, source_target_pairs={{0,4},{1,5},{2,6},{3,7},{16,20},{17,21},{18,22},{19,23}} | collective-permute-start | bytes 983048 | tf_op jit(solution)/shard_map/ppermute | solution.py:339
  70.7 19.0 %collective-permute-start.1 = (f32[4,320,128]{2,1,0:T(8,128)S(1)}, f32[4,320,128]{2,1,0:T(8,128)S(1)}, u32[]{:S(2)}, u32[]{:S(2)}) collective-permute-start(f32[4,320,128]{2,1,0:T(8,128)S(1)} %slice_add_fusion.2), channel_id=1, source_target_pairs={{0,2},{1,3},{2,0},{3,1},{4,6},{5,7},{6,4},{7,5},{8,10},{9,11},{10,... | collective-permute-start | bytes 1966088 | tf_op jit(solution)/shard_map/ppermute | solution.py:339
  74.9 30.2 %collective-permute-start.11 = (f32[8,320,128]{2,1,0:T(8,128)S(1)}, f32[8,320,128]{2,1,0:T(8,128)S(1)}, u32[]{:S(2)}, u32[]{:S(2)}) collective-permute-start(f32[8,320,128]{2,1,0:T(8,128)S(1)} %get-tuple-element.43), channel_id=1, source_target_pairs={{0,1},{1,0},{2,3},{3,2},{4,5},{5,4},{6,7},{7,6},{8,9},{9,8},{10,11... | collective-permute-start | bytes 3932168 | tf_op jit(solution)/shard_map/ppermute | solution.py:339
  76.0 25.7 %collective-permute-start.10 = (f32[4,320,128]{2,1,0:T(8,128)S(1)}, f32[4,320,128]{2,1,0:T(8,128)S(1)}, u32[]{:S(2)}, u32[]{:S(2)}) collective-permute-start(f32[4,320,128]{2,1,0:T(8,128)S(1)} %slice_add_fusion), channel_id=1, source_target_pairs={{0,2},{1,3},{2,0},{3,1},{4,6},{5,7},{6,4},{7,5},{8,10},{9,11},{10,... | collective-permute-start | bytes 1966088 | tf_op jit(solution)/shard_map/ppermute | solution.py:339
  89.9 15.1 %collective-permute-start.7 = (f32[320,128]{1,0:T(8,128)S(1)}, f32[320,128]{1,0:T(8,128)S(1)}, u32[]{:S(2)}, u32[]{:S(2)}) collective-permute-start(f32[320,128]{1,0:T(8,128)S(1)} %get-tuple-element.59), channel_id=1, source_target_pairs={{0,8},{1,9},{2,10},{3,11},{4,12},{5,13},{6,14},{7,15},{8,0},{9,1},... | collective-permute-start | bytes 491528 | tf_op jit(solution)/shard_map/ppermute | solution.py:339
  90.0 15.1 %collective-permute-start.8 = (f32[320,128]{1,0:T(8,128)S(1)}, f32[320,128]{1,0:T(8,128)S(1)}, u32[]{:S(2)}, u32[]{:S(2)}) collective-permute-start(f32[320,128]{1,0:T(8,128)S(1)} %get-tuple-element.60), channel_id=1, source_target_pairs={{0,12},{1,13},{2,14},{3,15},{4,8},{5,9},{6,10},{7,11},{8,4},{9,5},... | collective-permute-start | bytes 491528 | tf_op jit(solution)/shard_map/ppermute | solution.py:339
  94.8 10.2 %collective-permute-start.6 = (f32[320,128]{1,0:T(8,128)S(1)}, f32[320,128]{1,0:T(8,128)S(1)}, u32[]{:S(2)}, u32[]{:S(2)}) collective-permute-start(f32[320,128]{1,0:T(8,128)S(1)} %get-tuple-element.61), channel_id=1, source_target_pairs={{0,4},{1,5},{2,6},{3,7},{4,0},{5,1},{6,2},{7,3},{8,12},{9,13},{10,... | collective-permute-start | bytes 491528 | tf_op jit(solution)/shard_map/ppermute | solution.py:339
  105.1 29.1 %copy-start.4 = (bf16[1280,1440]{1,0:T(8,128)(2,1)S(1)}, bf16[1280,1440]{1,0:T(8,128)(2,1)}, u32[]{:S(2)}) copy-start(bf16[1280,1440]{1,0:T(8,128)(2,1)} %copy-done.3) | copy-start | bytes 11059204
  105.2 16.8 %collective-permute-start.16 = (f32[4,320,128]{2,1,0:T(8,128)S(1)}, f32[4,320,128]{2,1,0:T(8,128)S(1)}, u32[]{:S(2)}, u32[]{:S(2)}) collective-permute-start(f32[4,320,128]{2,1,0:T(8,128)S(1)} %slice_add_fusion.4), channel_id=1, source_target_pairs={{0,2},{1,3},{2,0},{3,1},{4,6},{5,7},{6,4},{7,5},{8,10},{9,11},{10,... | collective-permute-start | bytes 1966088 | tf_op jit(solution)/shard_map/ppermute | solution.py:339
  105.3 16.6 %collective-permute-start.15 = (f32[320,128]{1,0:T(8,128)S(1)}, f32[320,128]{1,0:T(8,128)S(1)}, u32[]{:S(2)}, u32[]{:S(2)}) collective-permute-start(f32[320,128]{1,0:T(8,128)S(1)} %slice_bitcast_fusion.5), channel_id=1, source_target_pairs={{0,2},{1,3},{2,0},{3,1},{4,6},{5,7},{6,4},{7,5},{8,10},{9,11},{10,... | collective-permute-start | bytes 491528 | tf_op jit(solution)/shard_map/ppermute | solution.py:339
  107.3 14.6 %collective-permute-start.13 = (f32[320,128]{1,0:T(8,128)S(1)}, f32[320,128]{1,0:T(8,128)S(1)}, u32[]{:S(2)}, u32[]{:S(2)}) collective-permute-start(f32[320,128]{1,0:T(8,128)S(1)} %get-tuple-element.62), channel_id=1, source_target_pairs={{0,8},{1,9},{2,10},{3,11},{4,12},{5,13},{6,14},{7,15},{8,0},{9,1},... | collective-permute-start | bytes 491528 | tf_op jit(solution)/shard_map/ppermute | solution.py:339
  111.7 10.2 %collective-permute-start.14 = (f32[320,128]{1,0:T(8,128)S(1)}, f32[320,128]{1,0:T(8,128)S(1)}, u32[]{:S(2)}, u32[]{:S(2)}) collective-permute-start(f32[320,128]{1,0:T(8,128)S(1)} %get-tuple-element.63), channel_id=1, source_target_pairs={{0,12},{1,13},{2,14},{3,15},{4,8},{5,9},{6,10},{7,11},{8,4},{9,5},... | collective-permute-start | bytes 491528 | tf_op jit(solution)/shard_map/ppermute | solution.py:339
  113.0 8.9 %collective-permute-start.12 = (f32[320,128]{1,0:T(8,128)S(1)}, f32[320,128]{1,0:T(8,128)S(1)}, u32[]{:S(2)}, u32[]{:S(2)}) collective-permute-start(f32[320,128]{1,0:T(8,128)S(1)} %get-tuple-element.64), channel_id=1, source_target_pairs={{0,4},{1,5},{2,6},{3,7},{4,0},{5,1},{6,2},{7,3},{8,12},{9,13},{10,... | collective-permute-start | bytes 491528 | tf_op jit(solution)/shard_map/ppermute | solution.py:339
  122.2 15.1 %collective-permute-start.18 = (f32[320,128]{1,0:T(8,128)S(1)}, f32[320,128]{1,0:T(8,128)S(1)}, u32[]{:S(2)}, u32[]{:S(2)}) collective-permute-start(f32[320,128]{1,0:T(8,128)S(1)} %get-tuple-element.56), channel_id=1, source_target_pairs={{0,8},{1,9},{2,10},{3,11},{4,12},{5,13},{6,14},{7,15},{16,24},{17,... | collective-permute-start | bytes 491528 | tf_op jit(solution)/shard_map/ppermute | solution.py:339
  130.4 8.1 %collective-permute-start.19 = (f32[320,128]{1,0:T(8,128)S(1)}, f32[320,128]{1,0:T(8,128)S(1)}, u32[]{:S(2)}, u32[]{:S(2)}) collective-permute-start(f32[320,128]{1,0:T(8,128)S(1)} %get-tuple-element.57), channel_id=1, source_target_pairs={{0,12},{1,13},{2,14},{3,15},{4,8},{5,9},{6,10},{7,11},{16,28},{17,... | collective-permute-start | bytes 491528 | tf_op jit(solution)/shard_map/ppermute | solution.py:339
  131.7 8.5 %collective-permute-start.17 = (f32[320,128]{1,0:T(8,128)S(1)}, f32[320,128]{1,0:T(8,128)S(1)}, u32[]{:S(2)}, u32[]{:S(2)}) collective-permute-start(f32[320,128]{1,0:T(8,128)S(1)} %get-tuple-element.58), channel_id=1, source_target_pairs={{0,4},{1,5},{2,6},{3,7},{4,0},{5,1},{6,2},{7,3},{16,20},{17,21},{1... | collective-permute-start | bytes 491528 | tf_op jit(solution)/shard_map/ppermute | solution.py:339
  (9 other events, 37.6 us)
